TPU v7x, 32 devices: a whole 2x2x4 slice. The times are simulated.
32 devices in a mesh: node: 8 (over z, y), local: 4 (over x, core).
Axes of the slice: x: 2, y: 2, z: 4, core: 2. Of those that a mesh axis runs over, the one named last changes fastest.
Arguments:
- hidden: bfloat16 [4096, 3584], P(('node', 'local')), may hold values from -6 to 6
- latent_weight: bfloat16 [3584, 576], P('node'), may hold values from -0.09375 to 0.09375
- latent_gain: float32 [512], replicated, may hold values from 0.1 to 1.9
- queries: bfloat16 [4096, 12288], P(('node', 'local')), may hold values from -200 to 200
- kv_weight: bfloat16 [512, 16384], P('node', 'local'), may hold values from -0.25 to 0.25
- expert_ids: int32 [4096, 8], P(('node', 'local')), may hold values from 0 to 255, as said below
- route_weights: float32 [4096, 8], P(('node', 'local')), may hold values from 0.05 to 0.6
- gate_proj: bfloat16 [32, 3584, 512], P(('node', 'local')), may hold values from -0.09375 to 0.09375
- up_proj: bfloat16 [32, 3584, 512], P(('node', 'local')), may hold values from -0.09375 to 0.09375
- down_proj: bfloat16 [32, 512, 3584], P(('node', 'local')), may hold values from -0.1875 to 0.1875
Outputs:
- attention: bfloat16 [4096, 8192], P(('node', 'local'))
- routed: bfloat16 [4096, 3584], P(('node', 'local'))
Inputs may be any that keep to these rules, and one draw needn't show every extreme that they name: `expert_ids`: each row names 8 different experts, all of them in at most 4 of the 8 groups of 32 consecutive expert numbers.
All inputs are finite; a program needn't handle non-finite values.
Results may differ from a plain program's by a relative error of at most 0.014.
The roundings to bfloat16 on the way count: a program that leaves them out, or rounds other values in their place, can miss the bound.
Values may be sent and summed in bfloat16 or wider, within the bound.
A program may use at most 128 MiB of HBM per device.

v0:
```python
import math

import jax
import jax.numpy as jnp
from jax import lax
from jax.sharding import PartitionSpec as P

NOPE = 128
ROPE = 64
VDIM = 128
LAT = 512
EXPERTS = 256
TOPK = 8
CAP = 8


def normalize(columns, latent_gain):
    mean_square = jnp.mean(columns * columns, axis=1, keepdims=True)
    return (columns * lax.rsqrt(mean_square + 1e-06) * latent_gain[None, :]).astype(jnp.bfloat16)


def rotate_keys(rope_part, position):
    half_width = ROPE // 2
    freqs = 10000.0 ** (-2.0 * jnp.arange(half_width, dtype=jnp.float32) / ROPE)
    angles = position.astype(jnp.float32)[:, None] * freqs[None, :]
    cosine = jnp.cos(angles)
    sine = jnp.sin(angles)
    first_half = rope_part[:, :half_width]
    second_half = rope_part[:, half_width:]
    return jnp.concatenate(
        [first_half * cosine - second_half * sine, second_half * cosine + first_half * sine], axis=1
    )


def attend_head(query_rows, keyval, keys_rope):
    length = query_rows.shape[0]
    q_block = min(length, 512)
    keys_nope = keyval[:, :NOPE]
    values = keyval[:, NOPE:]
    scale = 1.0 / math.sqrt(NOPE + ROPE)

    def one_block(block_index):
        offset = block_index * q_block
        block_rows = lax.dynamic_slice_in_dim(query_rows, offset, q_block, 0)
        scores = jnp.einsum(
            "qd,kd->qk", block_rows[:, :NOPE], keys_nope, preferred_element_type=jnp.float32
        )
        scores = scores + jnp.einsum(
            "qd,kd->qk", block_rows[:, NOPE:], keys_rope, preferred_element_type=jnp.float32
        )
        scores = scores * scale
        query_pos = offset + jnp.arange(q_block, dtype=jnp.int32)[:, None]
        key_pos = jnp.arange(length, dtype=jnp.int32)[None, :]
        scores = jnp.where(key_pos <= query_pos, scores, -1e30)
        row_max = jnp.max(scores, axis=1, keepdims=True)
        weights = jnp.exp(scores - row_max)
        probs = (weights / jnp.sum(weights, axis=1, keepdims=True)).astype(jnp.bfloat16)
        return jnp.dot(probs, values, preferred_element_type=jnp.float32).astype(jnp.bfloat16)

    blocks = lax.map(one_block, jnp.arange(length // q_block, dtype=jnp.int32))
    return blocks.reshape(length, values.shape[1])


def send_rows(buffer):
    return lax.all_to_all(buffer, ("node", "local"), split_axis=0, concat_axis=0, tiled=True)


def return_rows(buffer):
    return lax.all_to_all(buffer, ("node", "local"), split_axis=0, concat_axis=0, tiled=True)


def expert_half(row_block, gate_proj, up_proj, down_proj):
    stacked = row_block.reshape(-1, row_block.shape[-1])
    gate = jnp.dot(stacked, gate_proj[0], preferred_element_type=jnp.float32)
    upper = jnp.dot(stacked, up_proj[0], preferred_element_type=jnp.float32)
    inner = (jax.nn.silu(gate) * upper).astype(jnp.bfloat16)
    return (
        jnp.dot(inner, down_proj[0], preferred_element_type=jnp.float32)
        .astype(jnp.bfloat16)
        .reshape(row_block.shape)
    )


def shards(
    hidden,
    latent_weight,
    latent_gain,
    queries,
    kv_weight,
    expert_ids,
    route_weights,
    gate_proj,
    up_proj,
    down_proj,
):
    tok_rows = hidden.shape[0]
    width = hidden.shape[1]
    devices = lax.axis_size("node") * lax.axis_size("local")
    columns = hidden
    latent = jnp.dot(
        columns,
        lax.all_gather(latent_weight, "node", axis=0, tiled=True),
        preferred_element_type=jnp.float32,
    )
    position = lax.axis_index("local") * tok_rows + jnp.arange(tok_rows, dtype=jnp.int32)
    compressed = normalize(latent[:, :LAT], latent_gain)
    rope_keys = rotate_keys(latent[:, LAT:], position).astype(jnp.bfloat16)
    sequence = lax.all_gather(
        jnp.concatenate([compressed, rope_keys], axis=1), "local", axis=0, tiled=True
    )
    length = sequence.shape[0]
    head_queries = lax.all_to_all(queries, "local", split_axis=1, concat_axis=0, tiled=True)
    heads_here = head_queries.shape[1] // (NOPE + ROPE)
    portion = lax.all_gather(kv_weight, "node", axis=0, tiled=True)
    columns = lax.slice_in_dim(sequence, 0, portion.shape[0], axis=1)
    keyval = jnp.dot(columns, portion, preferred_element_type=jnp.float32).astype(jnp.bfloat16)
    keys_rope = sequence[:, LAT:]
    query_stack = head_queries.reshape(length, heads_here, NOPE + ROPE).transpose(1, 0, 2)
    keyval_stack = keyval.reshape(length, heads_here, NOPE + VDIM).transpose(1, 0, 2)
    outputs = lax.map(
        lambda head_pair: attend_head(head_pair[0], head_pair[1], keys_rope),
        (query_stack, keyval_stack),
    )
    merged = outputs.transpose(1, 0, 2).reshape(length, heads_here * VDIM)
    attention = lax.all_to_all(merged, "local", split_axis=0, concat_axis=1, tiled=True)
    flight = devices // 2
    stride = EXPERTS // flight
    routes_flat = expert_ids.reshape(-1)
    in_flight = routes_flat % stride == 0
    target = routes_flat // stride
    onehot = (
        (target[:, None] == jnp.arange(flight, dtype=jnp.int32)[None, :]) & in_flight[:, None]
    ).astype(jnp.int32)
    slot_index = jnp.sum((jnp.cumsum(onehot, axis=0) - onehot) * onehot, axis=1)
    kept_mask = in_flight & (slot_index < CAP)
    dump_slot = flight * CAP
    place_index = jnp.where(kept_mask, target * CAP + slot_index, dump_slot)
    token_index = jnp.arange(routes_flat.shape[0], dtype=jnp.int32) // TOPK
    row_table = (
        jnp.full((dump_slot + 1,), tok_rows, jnp.int32).at[place_index].set(token_index)[:dump_slot]
    )
    padded = jnp.concatenate([hidden, jnp.zeros((1, width), jnp.bfloat16)], axis=0)
    outgoing = padded[row_table].reshape(flight, CAP, width)
    doubled = jnp.broadcast_to(outgoing[:, None], (flight, 2, CAP, width)).reshape(
        devices, CAP, width
    )
    arrived = send_rows(doubled)
    partial_value = expert_half(arrived, gate_proj, up_proj, down_proj)
    returned = return_rows(partial_value).reshape(flight, 2, CAP, width)
    results = (returned[:, 0].astype(jnp.float32) + returned[:, 1].astype(jnp.float32)).astype(
        jnp.bfloat16
    )
    results = results.reshape(flight * CAP, width)
    results = jnp.concatenate([results, jnp.zeros((1, width), jnp.bfloat16)], axis=0)
    route_index = place_index.reshape(tok_rows, TOPK)
    routed = jnp.zeros((tok_rows, width), jnp.float32)
    for column in range(TOPK):
        routed = routed + route_weights[:, column : column + 1] * results[
            route_index[:, column]
        ].astype(jnp.float32)
    return (attention, routed.astype(jnp.bfloat16))


def solution(mesh):
    placed = (
        P(("node", "local"), None),
        P("node", None),
        P(),
        P(("node", "local"), None),
        P("node", "local"),
        P(("node", "local"), None),
        P(("node", "local"), None),
        P(("node", "local"), None, None),
        P(("node", "local"), None, None),
        P(("node", "local"), None, None),
    )
    return jax.shard_map(
        shards,
        mesh=mesh,
        in_specs=placed,
        out_specs=(P(("node", "local"), None), P(("node", "local"), None)),
        check_vma=False,
    )
```

profile of v0, /device:TPU:1, one launch (start us, length us, event | category | flops | bytes accessed | tf_op | source)
XLA Modules:
  0.0 332.2 jit_solution(9985815792288593533)
XLA Ops:
  7.9 4.7 %copy.52 = bf16[128,12288]{0,1:T(8,128)(2,1)} copy(bf16[128,12288]{1,0:T(8,128)(2,1)} %param.15) | data formatting | bytes 6291456 | tf_op args[3]
  12.6 4.9 %all-to-all-start = ((bf16[128,4,3072]{0,2,1:T(8,128)(2,1)}), bf16[128,4,3072]{0,2,1:T(8,128)(2,1)}, u32[]{:S(2)}, u32[]{:S(2)}) async-start(bf16[128,4,3072]{0,2,1:T(8,128)(2,1)} %bitcast.3), calls=%async_computation | async-start | bytes 6291456 | tf_op jit(solution)/shard_map/all_to_all | solution.py:112
  18.7 4.5 %reduce-window.6 = s32[16,8,128]{2,1,0:T(8,128)S(1)} reduce-window(s32[16,8,128]{2,1,0:T(8,128)S(1)} %fusion.59, s32[]{:T(128)} %copy.88), window={size=1x1x128 pad=0_0x0_0x127_0}, to_apply=%region_5.6 | reduce-window | flops 2080768 | bytes 131076 | tf_op jit(solution)/shard_map/reduce-window
  23.8 4.3 %scatter_custom_fusion = s32[129]{0:T(256)S(1)} fusion(s32[1024]{0:T(1024)S(1)} %bitcast.123, s32[1024]{0:T(1024)S(1)} %add_select_fusion.2, s32[]{:T(128)} %constant.132.clone.1), kind=kCustom, calls=%fused_computation.155 | custom fusion | bytes 520 | tf_op jit(solution)/shard_map/scatter | solution.py:140
  29.2 24.5 %all-to-all-done = bf16[128,4,3072]{0,2,1:T(8,128)(2,1)} async-done(((bf16[128,4,3072]{0,2,1:T(8,128)(2,1)}), bf16[128,4,3072]{0,2,1:T(8,128)(2,1)}, u32[]{:S(2)}, u32[]{:S(2)}) %all-to-all-start) | async-done | bytes 3145760 | tf_op jit(solution)/shard_map/all_to_all | solution.py:112
  55.2 6.9 %all-to-all-start.2 = ((bf16[32,8,3584]{2,1,0:T(8,128)(2,1)}), bf16[32,8,3584]{2,1,0:T(8,128)(2,1)}, u32[]{:S(2)}, u32[]{:S(2)}) async-start(bf16[32,8,3584]{2,1,0:T(8,128)(2,1)} %bitcast.16), calls=%async_computation.2 | async-start | bytes 3670016 | tf_op jit(solution)/shard_map/all_to_all | solution.py:65
  62.8 4.7 %copy.53 = bf16[4,128,3072]{1,0,2:T(4,128)(2,1)S(1)} copy(bf16[4,128,3072]{1,2,0:T(8,128)(2,1)} %bitcast.4) | data formatting | bytes 6291456 | tf_op jit(solution)/shard_map/all_to_all | solution.py:112
  67.5 3.3 reshape.245
  70.8 56.5 %all-to-all-done.2 = bf16[32,8,3584]{2,1,0:T(8,128)(2,1)} async-done(((bf16[32,8,3584]{2,1,0:T(8,128)(2,1)}), bf16[32,8,3584]{2,1,0:T(8,128)(2,1)}, u32[]{:S(2)}, u32[]{:S(2)}) %all-to-all-start.2) | async-done | bytes 1835040 | tf_op jit(solution)/shard_map/all_to_all | solution.py:65
  127.3 4.0 %fusion.16 = f32[256,512]{1,0:T(8,128)S(1)} fusion(bf16[1,3584,512]{2,1,0:T(8,128)(2,1)} %param.19, bf16[32,8,3584]{2,1,0:T(8,128)(2,1)} %all-to-all-done.2), kind=kOutput, calls=%fused_computation.36 | convolution fusion | flops 939524096 | bytes 6029312 | tf_op jit(solution)/shard_map/dot_general | solution.py:74
  131.3 7.2 %fusion.12 = bf16[32,8,3584]{2,1,0:T(8,128)(2,1)} fusion(bf16[1,512,3584]{2,1,0:T(8,128)(2,1)} %param.21, bf16[1,3584,512]{2,1,0:T(8,128)(2,1)} %param.20, bf16[32,8,3584]{2,1,0:T(8,128)(2,1)} %all-to-all-done.2, f32[256,512]{1,0:T(8,128)S(1)} %fusion.16), kind=kOutput, calls=%fused_computation.31 | convolution fusion | flops 1880752128 | bytes 11534336 | tf_op jit(solution)/shard_map/dot_general | solution.py:78
  138.5 3.7 %all-to-all-start.3 = ((bf16[32,8,3584]{2,1,0:T(8,128)(2,1)}), bf16[32,8,3584]{2,1,0:T(8,128)(2,1)}, u32[]{:S(2)}, u32[]{:S(2)}) async-start(bf16[32,8,3584]{2,1,0:T(8,128)(2,1)} %fusion.12), calls=%async_computation.3 | async-start | bytes 3670016 | tf_op jit(solution)/shard_map/all_to_all | solution.py:69
  142.3 4.1 %fusion.84 = f32[128,576]{0,1:T(8,128)S(1)} fusion(bf16[128,3584]{1,0:T(8,128)(2,1)S(1)} %copy-done.1, bf16[3584,576]{1,0:T(8,128)(2,1)} %all-gather.3.cloned.1.call-done), kind=kOutput, calls=%fused_computation.163 | convolution fusion | flops 528482304 | bytes 5341184 | tf_op jit(solution)/shard_map/dot_general | solution.py:100
  146.8 14.4 %all_gather.10 = bf16[512,576]{0,1:T(8,128)(2,1)S(1)} all-gather(bf16[128,576]{0,1:T(8,128)(2,1)S(1)} %pad_maximum_fusion), channel_id=1, replica_groups=mesh['node'=8,'local'=4] {'local'}, dimensions={0}, use_global_device_ids=true | all-gather | bytes 737280 | tf_op jit(solution)/shard_map/all_gather | solution.py:108
  161.3 61.9 %all-gather.5.cloned.1.call-done = bf16[512,4096]{1,0:T(8,128)(2,1)} async-done(((bf16[64,4096]{1,0:T(8,128)(2,1)}), bf16[512,4096]{1,0:T(8,128)(2,1)}) %all-gather.5.cloned.1.call-update) | async-done | bytes 4194320 | tf_op jit(solution)/shard_map/all_gather | solution.py:114
  223.2 4.6 %convolution_convert_fusion.1 = bf16[512,4096]{1,0:T(8,128)(2,1)S(1)} fusion(bf16[512,4096]{1,0:T(8,128)(2,1)} %all-gather.5.cloned.1.call-done, bf16[512,576]{0,1:T(8,128)(2,1)S(1)} %all_gather.10), kind=kOutput, calls=%fused_computation.29 | convolution fusion | flops 2149580800 | bytes 8912896 | tf_op jit(solution)/shard_map/dot_general | solution.py:116
  227.8 2.3 copy.78
  230.1 53.2 %while.16 = (s32[]{:T(128)}, bf16[16,512,128]{2,1,0:T(8,128)(2,1)S(1)}, bf16[16,512,192]{1,2,0:T(8,128)(2,1)}, bf16[16,512,256]{2,1,0:T(8,128)(2,1)}, bf16[512,64]{1,0:T(8,128)(2,1)S(1)}, /*index=5*/s32[]{:T(128)}) while((s32[]{:T(128)}, bf16[16,512,128]{2,1,0:T(8,128)(2,1)S(1)}, bf16[16,512,192]{1,2,0:T(8,128)(2,1)}, ...), condition=%wide.region_4.5_spmd, body=%wide.region_1.4_spmd.sunk | while | flops 170458112 | bytes 7350353 | solution.py:120
  284.7 2.9 copy.57
  287.6 2.3 all_to_all.35
  289.9 4.0 %all-to-all-start.1 = ((bf16[4,128,2048]{2,1,0:T(8,128)(2,1)}), bf16[4,128,2048]{2,1,0:T(8,128)(2,1)S(1)}, u32[]{:S(2)}, u32[]{:S(2)}) async-start(bf16[4,128,2048]{2,1,0:T(8,128)(2,1)} %all_to_all.35), calls=%async_computation.1 | async-start | bytes 4194304 | tf_op jit(solution)/shard_map/all_to_all | solution.py:125
  295.7 2.1 gather_fusion.1
  297.7 2.0 gather_fusion.2
  299.8 2.0 gather_fusion.3
  301.8 2.1 gather_fusion.4
  303.9 2.0 gather_fusion.5
  305.9 2.1 gather_fusion.6
  308.0 2.0 gather_fusion.7
  310.1 2.0 gather_fusion.8
  312.1 5.7 %add_convert_fusion = bf16[128,3584]{1,0:T(8,128)(2,1)} fusion(bf16[128,3584]{1,0:T(8,128)(2,1)} %gather_fusion.8, bf16[128,3584]{1,0:T(8,128)(2,1)} %gather_fusion.7, bf16[128,3584]{1,0:T(8,128)(2,1)} %gather_fusion.6, bf16[128,3584]{1,0:T(8,128)(2,1)} %gather_fusion.5, bf16[128,3584]{1,0:T(8,128)(2,1)} %gather_fusion.4, ...), kind=kLoop, calls=%fused_computation.40 | loop fusion | flops 11010048 | bytes 8261632 | tf_op jit(solution)/shard_map/convert_element_type | solution.py:161
  318.8 2.5 copy.58
  321.3 4.1 %copy.70 = bf16[128,8192]{1,0:T(8,128)(2,1)} copy(bf16[128,8192]{0,1:T(8,128)(2,1)} %bitcast.115) | data formatting | bytes 4194304
  (176 shorter events, 62.7 us)
Async XLA Ops:
  7.2 135.1 %all-gather.3.cloned.1.call-start = ((), (), s32[]{:S(2)}) async-start(), calls=%async_computation.4 | async-start | bytes 5160960 | tf_op jit(solution)/shard_map/all_gather | solution.py:102
  12.6 5.6 %copy-start.4 = (s32[128,8]{0,1:T(8,128)S(1)}, s32[128,8]{0,1:T(8,128)}, u32[]{:S(2)}) copy-start(s32[128,8]{0,1:T(8,128)} %param.17) | copy-start | bytes 12292
  12.6 41.2 %all-to-all-start = ((bf16[128,4,3072]{0,2,1:T(8,128)(2,1)}), bf16[128,4,3072]{0,2,1:T(8,128)(2,1)}, u32[]{:S(2)}, u32[]{:S(2)}) async-start(bf16[128,4,3072]{0,2,1:T(8,128)(2,1)} %bitcast.3), calls=%async_computation | async-start | bytes 6291456 | tf_op jit(solution)/shard_map/all_to_all | solution.py:112
  17.5 6.0 %copy-start = (bf16[128,3584]{1,0:T(8,128)(2,1)S(1)}, bf16[128,3584]{1,0:T(8,128)(2,1)}, u32[]{:S(2)}) copy-start(bf16[128,3584]{1,0:T(8,128)(2,1)} %param.12) | copy-start | bytes 2752516
  17.5 205.7 %all-gather.5.cloned.1.call-start = ((), (), s32[]{:S(2)}) async-start(), calls=%async_computation.5 | async-start | bytes 4718592 | tf_op jit(solution)/shard_map/all_gather | solution.py:114
  55.2 7.5 %copy-start.5 = (f32[128,8]{0,1:T(8,128)S(1)}, f32[128,8]{0,1:T(8,128)}, u32[]{:S(2)}) copy-start(f32[128,8]{0,1:T(8,128)} %param.18) | copy-start | bytes 12292
  55.2 72.0 %all-to-all-start.2 = ((bf16[32,8,3584]{2,1,0:T(8,128)(2,1)}), bf16[32,8,3584]{2,1,0:T(8,128)(2,1)}, u32[]{:S(2)}, u32[]{:S(2)}) async-start(bf16[32,8,3584]{2,1,0:T(8,128)(2,1)} %bitcast.16), calls=%async_computation.2 | async-start | bytes 3670016 | tf_op jit(solution)/shard_map/all_to_all | solution.py:65
  138.5 3.8 %copy-start.1 = (bf16[128,3584]{1,0:T(8,128)(2,1)S(1)}, bf16[128,3584]{1,0:T(8,128)(2,1)}, u32[]{:S(2)}) copy-start(bf16[128,3584]{1,0:T(8,128)(2,1)} %param.12) | copy-start | bytes 2752516
  138.5 151.4 %all-to-all-start.3 = ((bf16[32,8,3584]{2,1,0:T(8,128)(2,1)}), bf16[32,8,3584]{2,1,0:T(8,128)(2,1)}, u32[]{:S(2)}, u32[]{:S(2)}) async-start(bf16[32,8,3584]{2,1,0:T(8,128)(2,1)} %fusion.12), calls=%async_computation.3 | async-start | bytes 3670016 | tf_op jit(solution)/shard_map/all_to_all | solution.py:69
  142.2 4.4 %copy-start.6 = (f32[512]{0:T(512)S(1)}, f32[512]{0:T(512)}, u32[]{:S(2)}) copy-start(f32[512]{0:T(512)} %param.14) | copy-start | bytes 6148
  227.8 2.4 copy-start.2
  283.3 1.3 copy-start.3
  289.9 28.9 %all-to-all-start.1 = ((bf16[4,128,2048]{2,1,0:T(8,128)(2,1)}), bf16[4,128,2048]{2,1,0:T(8,128)(2,1)S(1)}, u32[]{:S(2)}, u32[]{:S(2)}) async-start(bf16[4,128,2048]{2,1,0:T(8,128)(2,1)} %all_to_all.35), calls=%async_computation.1 | async-start | bytes 4194304 | tf_op jit(solution)/shard_map/all_to_all | solution.py:125
Sparse Core Ops, SparseCore 0:
  10.2 104.9 all-gather.2
  117.3 105.8 all-gather.4
where the time goes:
time: 335 us; the launch traced here: 332 us
  waiting for transfers between devices  145 us (43%)
  local copies, waits for them, and re-layouts  85.3 us (25%)
  matrix products  36.5 us (11%)
  starting transfers between devices  19.5 us (6%)
  other arithmetic  16.2 us (5%)
  blocking collectives  14.4 us (4%)
  between operations  14.4 us (4%)
    all_gather x1, waiting for transfers between devices, shards(): portion = lax.all_gather(kv_weight, 'node', axis=0, tiled=True)  61.9 us
    all_to_all x1, waiting for transfers between devices, send_rows(): lax.all_to_all(buffer, ('node', 'local'), split_axis=0, concat_axis=0, ti...  56.5 us
    all_to_all x1, waiting for transfers between devices, shards(): lax.all_to_all(queries, 'local', split_axis=1, concat_axis=0, tiled=True)  24.5 us
    dynamic_slice x32, local copies, waits for them, and re-layouts, shards(): lax.map(lambda head_pair: attend_head(head_pair[0], head_pair[1], keys_ro...  17.2 us
    gather x8, local copies, waits for them, and re-layouts, shards(): results[route_index[:, column]].astype(jnp.float32)  16.4 us
    squeeze x16, local copies, waits for them, and re-layouts, shards(): lax.map(lambda head_pair: attend_head(head_pair[0], head_pair[1], keys_ro...  15.6 us
    all_gather x1, blocking collectives, shards(): lax.all_gather(jnp.concatenate([compressed, rope_keys], axis=1), 'local',...  14.4 us
    unnamed x17, local copies, waits for them, and re-layouts  10.2 us
  transfers between devices with their start and end apart: 6, of which 4 were waited for; matrix products, arithmetic and copies ran while one was open for 38% of the time, Pallas kernels for 0%

commit v1 on v0

v1 whole, which is shorter than its diff:
```python
import functools
import math

import jax
import jax.numpy as jnp
from jax import lax
from jax.experimental import pallas as pl
from jax.experimental.pallas import tpu as pltpu
from jax.sharding import PartitionSpec as P

NOPE = 128
ROPE = 64
VDIM = 128
LAT = 512
EXPERTS = 256
CAP = 8
PAIR_Q = 2 * (NOPE + ROPE)
PAIR_KV = 2 * (NOPE + VDIM)
PAIR_V = 2 * VDIM
MESH = pl.DeviceIdType.MESH
VMEM_LIMIT = 56 * 2**20


def remote(src, dst, send_sem, recv_sem, device):
    return pltpu.make_async_remote_copy(
        src_ref=src,
        dst_ref=dst,
        send_sem=send_sem,
        recv_sem=recv_sem,
        device_id=device,
        device_id_type=MESH,
    )


def greet(devices, n_local, me):
    barrier = pltpu.get_barrier_semaphore()

    def signal(d, carry):
        other = lax.rem(me + d, devices)
        pl.semaphore_signal(
            barrier,
            inc=1,
            device_id=(lax.div(other, n_local), lax.rem(other, n_local)),
            device_id_type=MESH,
        )
        return carry

    lax.fori_loop(1, devices, signal, 0)
    pl.semaphore_wait(barrier, devices - 1)


class Gather:
    def __init__(self, own, slot, nz, ny, node, local, sems):
        self.own, self.slot, self.nz, self.ny = own, slot, nz, ny
        self.z, self.y, self.local = lax.div(node, ny), lax.rem(node, ny), local
        self.up_s, self.up_r, self.dn_s, self.dn_r, self.y_s, self.y_r = sems

    def up(self, h, src):
        z = jnp.maximum(self.z - h, 0)
        dst = self.slot(z * self.ny + self.y)
        to = jnp.minimum(self.z + 1, self.nz - 1)
        return remote(
            dst if src is None else src, dst, self.up_s.at[h], self.up_r.at[h], (to * self.ny + self.y, self.local)
        )

    def down(self, h, src):
        z = jnp.minimum(self.z + h, self.nz - 1)
        dst = self.slot(z * self.ny + self.y)
        to = jnp.maximum(self.z - 1, 0)
        return remote(
            dst if src is None else src, dst, self.dn_s.at[h], self.dn_r.at[h], (to * self.ny + self.y, self.local)
        )

    def across(self, z, dy, src):
        dst = self.slot(z * self.ny + self.y)
        to = self.z * self.ny + lax.rem(self.y + dy, self.ny)
        return remote(
            dst if src is None else src, dst, self.y_s.at[z, dy - 1], self.y_r.at[z, dy - 1], (to, self.local)
        )

    def begin(self):
        @pl.when(self.z < self.nz - 1)
        def _():
            self.up(0, self.own).start()

        @pl.when(self.z > 0)
        def _():
            self.down(0, self.own).start()

        for dy in range(1, self.ny):
            self.across(self.z, dy, self.own).start()

    def hop(self, h, landed=None):
        @pl.when(self.z - h >= 0)
        def _():
            self.up(h - 1, None).wait_recv()
            if h < self.nz - 1:

                @pl.when(self.z < self.nz - 1)
                def _():
                    self.up(h, None).start()

            for dy in range(1, self.ny):
                self.across(self.z - h, dy, None).start()
            if landed:
                landed((self.z - h) * self.ny + self.y)

        @pl.when(self.z + h < self.nz)
        def _():
            self.down(h - 1, None).wait_recv()
            if h < self.nz - 1:

                @pl.when(self.z > 0)
                def _():
                    self.down(h, None).start()

            for dy in range(1, self.ny):
                self.across(self.z + h, dy, None).start()
            if landed:
                landed((self.z + h) * self.ny + self.y)

    def columns(self, landed=None):
        for z in range(self.nz):
            for dy in range(1, self.ny):
                self.across(z, dy, None).wait_recv()
                if landed:
                    landed(z * self.ny + lax.rem(self.y - dy + self.ny, self.ny))

    def finish(self):
        for h in range(self.nz - 1):

            @pl.when((self.z < self.nz - 1) & (self.z - h >= 0))
            def _():
                self.up(h, None).wait_send()

            @pl.when((self.z > 0) & (self.z + h < self.nz))
            def _():
                self.down(h, None).wait_send()

        for z in range(self.nz):
            for dy in range(1, self.ny):
                self.across(z, dy, None).wait_send()


def first_kernel(
    n_node,
    n_local,
    nz,
    hidden,
    pick,
    gain,
    cosine,
    sine,
    latent_w,
    queries,
    kv_w,
    gate_w,
    up_w,
    down_w,
    seq_out,
    q_out,
    kv_out,
    returned,
    lat,
    gates,
    ups,
    downs,
    leaving,
    arrived,
    part,
    sibpart,
    mine,
    local_sem,
    lat_sems,
    kv_sems,
    core_s,
    core_r,
    q_s,
    q_r,
    seq_s,
    seq_r,
    go_s,
    go_r,
    back_s,
    back_r,
    sib_s,
    sib_r,
):
    node, local = lax.axis_index("node"), lax.axis_index("local")
    devices, ny = n_node * n_local, n_node // nz
    chips = devices // 2
    me = node * n_local + local
    chip, core = lax.div(me, 2), lax.rem(me, 2)
    sibling = (node, local + 1 - 2 * core)
    half = lat.shape[2]
    tokens = hidden.shape[0]
    q_cols = q_out.shape[2]

    own_q = pl.ds(pl.multiple_of(local * q_cols, 128), q_cols)
    locals_ = [
        pltpu.make_async_copy(gate_w.at[0], gates, local_sem.at[0]),
        pltpu.make_async_copy(up_w.at[0], ups, local_sem.at[1]),
        pltpu.make_async_copy(down_w.at[0], downs, local_sem.at[2]),
        pltpu.make_async_copy(kv_w, kv_out.at[node], local_sem.at[3]),
        pltpu.make_async_copy(queries.at[:, own_q], q_out.at[local], local_sem.at[4]),
        pltpu.make_async_copy(latent_w.at[pl.ds(0, half)], lat.at[node, 0], local_sem.at[5]),
        pltpu.make_async_copy(latent_w.at[pl.ds(half, half)], lat.at[node, 1], local_sem.at[6]),
    ]
    for copy in locals_:
        copy.start()

    rows = jnp.dot(pick[...], hidden[...], preferred_element_type=jnp.float32)
    leaving[...] = rows.reshape(leaving.shape).astype(jnp.bfloat16)
    arrived[core, chip] = leaving[chip]

    greet(devices, n_local, me)

    def device_of(c):
        dev = c * 2 + core
        return (lax.div(dev, n_local), lax.rem(dev, n_local))

    def go(d):
        to = lax.rem(chip + d, chips)
        return remote(
            leaving.at[to], arrived.at[core, chip], go_s.at[d - 1], go_r.at[d - 1], device_of(to)
        )

    def back(d):
        to = lax.rem(chip + d, chips)
        return remote(
            part.at[core, to], returned.at[chip], back_s.at[d - 1], back_r.at[d - 1], device_of(to)
        )

    def each(first, last, act):
        def step(d, carry):
            act(d)
            return carry

        lax.fori_loop(first, last, step, 0)

    def ask(d):
        to = lax.rem(local + d, n_local)
        cols = pl.ds(pl.multiple_of(to * q_cols, 128), q_cols)
        return remote(
            queries.at[:, cols], q_out.at[local], q_s.at[d - 1], q_r.at[d - 1], (node, to)
        )

    lat_gather = Gather(
        latent_w.at[pl.ds(pl.multiple_of(core * half, 16), half)],
        lambda n: lat.at[n, core],
        nz,
        ny,
        node,
        local,
        lat_sems,
    )
    kv_gather = Gather(kv_w, lambda n: kv_out.at[n], nz, ny, node, local, kv_sems)

    def share(n):
        return remote(lat.at[n, core], lat.at[n, core], core_s.at[n], core_r.at[n], sibling)

    lat_gather.begin()
    each(1, chips, lambda d: go(d).start())
    kv_gather.begin()
    for d in range(1, n_local):
        ask(d).start()

    def landed(n):
        share(n).start()

    lat_gather.hop(1, landed)
    kv_gather.hop(1)
    lat_gather.hop(2, landed) if nz > 2 else None

    each(1, chips, lambda d: go(d).wait_recv())
    swap = remote(arrived.at[core], arrived.at[core], sib_s.at[0], sib_r.at[0], sibling)
    swap.start()
    for h in range(3, nz):
        lat_gather.hop(h, landed)
    if nz > 2:
        kv_gather.hop(2)
    for copy in locals_:
        copy.wait()
    swap.wait()

    block = 32
    per = chips // block if chips >= block else 1
    step_chips = min(block, chips)

    def expert(i, carry):
        c, p = lax.div(i, per), lax.rem(i, per)
        at = pl.ds(p * step_chips, step_chips)
        x = arrived[c, at].astype(jnp.float32).reshape(step_chips * CAP, -1).astype(jnp.bfloat16)
        gate = jnp.dot(x, gates[...], preferred_element_type=jnp.float32)
        upper = jnp.dot(x, ups[...], preferred_element_type=jnp.float32)
        inner = (gate / (1.0 + jnp.exp(-gate)) * upper).astype(jnp.bfloat16)
        width = downs.shape[1] // 7
        for j in range(7):
            cols = slice(j * width, (j + 1) * width)
            y = jnp.dot(inner, downs[:, cols], preferred_element_type=jnp.float32)
            part[c, at, :, cols] = y.reshape(step_chips, CAP, width).astype(jnp.bfloat16)
        return carry

    lax.fori_loop(0, 2 * per, expert, 0)
    give = remote(part.at[1 - core], sibpart, sib_s.at[1], sib_r.at[1], sibling)
    give.start()
    lat_gather.columns(landed)
    for h in range(3, nz):
        kv_gather.hop(h)
    give.wait()

    def total(p, carry):
        both = part[core, p].astype(jnp.float32) + sibpart[p].astype(jnp.float32)
        part[core, p] = both.astype(jnp.bfloat16)
        return carry

    lax.fori_loop(0, chips, total, 0)
    each(1, chips, lambda d: back(d).start())
    kept = pltpu.make_async_copy(part.at[core, chip], returned.at[chip], local_sem.at[7])
    kept.start()

    def other_half(n):
        return remote(
            lat.at[n, 1 - core], lat.at[n, 1 - core], core_s.at[n], core_r.at[n], sibling
        )

    def shared(n, carry):
        @pl.when(n != node)
        def _():
            other_half(n).wait_recv()

        return carry

    lax.fori_loop(0, n_node, shared, 0)
    weight = lat[...].reshape(n_node * 2 * half, lat.shape[3])
    latent = jnp.dot(hidden[...], weight, preferred_element_type=jnp.float32)
    u = latent[:, :LAT]
    scale = lax.rsqrt(jnp.mean(u * u, axis=1, keepdims=True) + 1e-06)
    mine[:, :LAT] = (u * scale * gain[...]).astype(jnp.bfloat16)
    a = latent[:, LAT:]
    swapped = jnp.concatenate([a[:, ROPE // 2 :], a[:, : ROPE // 2]], axis=1)
    mine[:, LAT:] = (a * cosine[...] + swapped * sine[...]).astype(jnp.bfloat16)

    def tell(d):
        to = lax.rem(local + d, n_local)
        return remote(mine, seq_out.at[local], seq_s.at[d - 1], seq_r.at[d - 1], (node, to))

    for d in range(1, n_local):
        tell(d).start()
    stays = pltpu.make_async_copy(mine, seq_out.at[local], local_sem.at[8])
    stays.start()

    kv_gather.columns()
    for d in range(1, n_local):
        ask(d).wait()
        tell(d).wait()
    each(1, chips, lambda d: back(d).wait())
    each(1, chips, lambda d: go(d).wait_send())
    kept.wait()
    stays.wait()
    lat_gather.finish()
    kv_gather.finish()

    def shared_sent(n, carry):
        @pl.when(n != node)
        def _():
            share(n).wait_send()

        return carry

    lax.fori_loop(0, n_node, shared_sent, 0)


def second_kernel(
    n_node, n_local, seq, queries, kv, results, combine, attention, routed, outs, send, recv, keep
):
    node, local = lax.axis_index("node"), lax.axis_index("local")
    devices = n_node * n_local
    me = node * n_local + local
    length = seq.shape[0]
    tokens = length // n_local
    pairs = kv.shape[1] // PAIR_KV
    wide = kv.shape[1] // 2
    scale = 1.0 / math.sqrt(NOPE + ROPE)
    step = 256

    barrier = pltpu.get_barrier_semaphore()
    for d in range(1, n_local):
        pl.semaphore_signal(
            barrier,
            inc=1,
            device_id=(node, lax.rem(local + d, n_local)),
            device_id_type=MESH,
        )

    def place(p):
        return pl.ds(pl.multiple_of(local * wide + p * PAIR_V, 128), PAIR_V)

    def tell(p, d):
        to = lax.rem(local + d, n_local)
        rows = pl.ds(pl.multiple_of(to * tokens, 16), tokens)
        return remote(
            outs.at[rows, pl.ds(pl.multiple_of(p * PAIR_V, 128), PAIR_V)],
            attention.at[:, place(p)],
            send.at[p, d - 1],
            recv.at[p, d - 1],
            (node, to),
        )

    def own(p):
        rows = pl.ds(pl.multiple_of(local * tokens, 16), tokens)
        return pltpu.make_async_copy(
            outs.at[rows, pl.ds(pl.multiple_of(p * PAIR_V, 128), PAIR_V)],
            attention.at[:, place(p)],
            keep.at[p],
        )

    compressed = seq[:, :LAT]
    rope = seq[:, LAT:].astype(jnp.float32)
    zeros = jnp.zeros((length, 128 - ROPE), jnp.float32)
    diagonal = lax.broadcasted_iota(jnp.int32, (step, step), 1) <= lax.broadcasted_iota(
        jnp.int32, (step, step), 0
    )

    def pair(p, carry):
        cols = pl.ds(pl.multiple_of(p * PAIR_KV, 128), PAIR_KV)
        keyval = jnp.dot(compressed, kv[:, cols], preferred_element_type=jnp.float32)
        first = jnp.concatenate([keyval[:, :NOPE], rope, zeros], axis=1).astype(jnp.bfloat16)
        at = NOPE + VDIM
        second = jnp.concatenate([zeros, keyval[:, at : at + NOPE], rope], axis=1).astype(
            jnp.bfloat16
        )
        for h, keys in enumerate((first, second)):
            values = keyval[:, h * at + NOPE : (h + 1) * at].astype(jnp.bfloat16)
            q_cols = pl.ds(pl.multiple_of(p * PAIR_Q + h * 128, 128), 256)
            for b in range(length // step):
                rows = slice(b * step, (b + 1) * step)
                end = (b + 1) * step
                scores = (
                    lax.dot_general(
                        queries[rows, q_cols],
                        keys[:end],
                        (((1,), (1,)), ((), ())),
                        preferred_element_type=jnp.float32,
                    )
                    * scale
                )
                last = jnp.where(diagonal, scores[:, b * step :], -1e30)
                scores = jnp.concatenate([scores[:, : b * step], last], axis=1) if b else last
                weights = jnp.exp(scores - jnp.max(scores, axis=1, keepdims=True))
                probs = (weights * (1.0 / jnp.sum(weights, axis=1, keepdims=True))).astype(
                    jnp.bfloat16
                )
                out = jnp.dot(probs, values[:end], preferred_element_type=jnp.float32)
                outs[rows, pl.ds(pl.multiple_of(p * PAIR_V + h * VDIM, 128), VDIM)] = out.astype(
                    jnp.bfloat16
                )

        @pl.when(p == 0)
        def _():
            pl.semaphore_wait(barrier, n_local - 1)

        for d in range(1, n_local):
            tell(p, d).start()
        own(p).start()
        return carry

    lax.fori_loop(0, pairs, pair, 0)

    rows = results[...].astype(jnp.float32).reshape(-1, results.shape[2]).astype(jnp.bfloat16)
    sums = jnp.dot(combine[0], rows, preferred_element_type=jnp.float32)
    for i in range(1, combine.shape[0]):
        sums += jnp.dot(combine[i], rows, preferred_element_type=jnp.float32)
    routed[...] = sums.astype(jnp.bfloat16)

    def settle(p, carry):
        for d in range(1, n_local):
            tell(p, d).wait()
        own(p).wait()
        return carry

    lax.fori_loop(0, pairs, settle, 0)


def shards(
    n_node,
    n_local,
    hidden,
    latent_weight,
    latent_gain,
    queries,
    kv_weight,
    expert_ids,
    route_weights,
    gate_proj,
    up_proj,
    down_proj,
):
    tokens, width = hidden.shape
    devices = n_node * n_local
    chips = devices // 2
    nz = 4 if n_node % 4 == 0 else n_node
    ny = n_node // nz
    bf16, f32 = jnp.bfloat16, jnp.float32

    present = jnp.arange(chips, dtype=jnp.int32) * (EXPERTS // chips)
    named = expert_ids[:, :, None] == present[None, None, :]
    member = jnp.any(named, axis=1)
    weight = jnp.sum(jnp.where(named, route_weights[:, :, None], 0.0), axis=1)
    at = jnp.arange(tokens, dtype=jnp.int32)
    earlier = (at[None, :] < at[:, None]).astype(bf16)
    slot = jnp.dot(earlier, member.astype(bf16), preferred_element_type=f32)
    slots = jnp.arange(CAP, dtype=jnp.int32).astype(f32)
    chosen = member[:, :, None] & (slot[:, :, None] == slots)
    pick = chosen.reshape(tokens, chips * CAP).astype(bf16).T
    dense = jnp.where(chosen, weight[:, :, None], 0.0).reshape(tokens, chips * CAP)
    high = lax.reduce_precision(dense, 8, 7)
    middle = lax.reduce_precision(dense - high, 8, 7)
    low = dense - high - middle
    combine = jnp.stack([high.astype(bf16), middle.astype(bf16), low.astype(bf16)])

    position = lax.axis_index("local") * tokens + at
    freqs = 10000.0 ** (-2.0 * jnp.arange(ROPE // 2, dtype=f32) / ROPE)
    angles = position.astype(f32)[:, None] * freqs[None, :]
    cosine, sine = jnp.cos(angles), jnp.sin(angles)
    cosine = jnp.concatenate([cosine, cosine], axis=1)
    sine = jnp.concatenate([-sine, sine], axis=1)

    half = latent_weight.shape[0] // 2
    total = latent_weight.shape[1]
    q_cols = queries.shape[1] // n_local
    vmem, hbm = pl.BlockSpec(memory_space=pltpu.VMEM), pl.BlockSpec(memory_space=pl.ANY)
    dma = pltpu.SemaphoreType.DMA
    chain = max(nz - 1, 1)
    gather = [dma((chain,))] * 4 + [dma((nz, max(ny - 1, 1)))] * 2
    others = max(n_local - 1, 1)
    width_e = gate_proj.shape[2]
    scratch = [
        pltpu.VMEM((n_node, 2, half, total), bf16),
        pltpu.VMEM((width, width_e), bf16),
        pltpu.VMEM((width, width_e), bf16),
        pltpu.VMEM((width_e, width), bf16),
        pltpu.VMEM((chips, CAP, width), bf16),
        pltpu.VMEM((2, chips, CAP, width), bf16),
        pltpu.VMEM((2, chips, CAP, width), bf16),
        pltpu.VMEM((chips, CAP, width), bf16),
        pltpu.VMEM((tokens, total), bf16),
        dma((9,)),
        *gather,
        *gather,
        dma((n_node,)),
        dma((n_node,)),
        *[dma((others,))] * 4,
        *[dma((chips - 1,))] * 4,
        dma((2,)),
        dma((2,)),
    ]

    def body(*refs):
        refs = list(refs)
        lat_sems, kv_sems = refs[25:31], refs[31:37]
        first_kernel(n_node, n_local, nz, *refs[:25], lat_sems, kv_sems, *refs[37:])

    sequence, head_queries, portion, results = pl.pallas_call(
        body,
        out_shape=(
            jax.ShapeDtypeStruct((n_local, tokens, total), bf16),
            jax.ShapeDtypeStruct((n_local, tokens, q_cols), bf16),
            jax.ShapeDtypeStruct((n_node, *kv_weight.shape), bf16),
            jax.ShapeDtypeStruct((chips, CAP, width), bf16),
        ),
        in_specs=[vmem] * 5 + [hbm] * 6,
        out_specs=(hbm,) * 4,
        scratch_shapes=scratch,
        compiler_params=pltpu.CompilerParams(
            collective_id=0, has_side_effects=True, vmem_limit_bytes=VMEM_LIMIT
        ),
        name="exchange",
    )(
        hidden,
        pick,
        latent_gain.reshape(1, -1),
        cosine,
        sine,
        latent_weight,
        queries,
        kv_weight,
        gate_proj,
        up_proj,
        down_proj,
    )

    length = n_local * tokens
    kv_cols = kv_weight.shape[1]
    pairs = kv_cols // PAIR_KV
    attention, routed = pl.pallas_call(
        functools.partial(second_kernel, n_node, n_local),
        out_shape=(
            jax.ShapeDtypeStruct((tokens, n_local * kv_cols // 2), bf16),
            jax.ShapeDtypeStruct((tokens, width), bf16),
        ),
        in_specs=[vmem] * 5,
        out_specs=(hbm, vmem),
        scratch_shapes=[
            pltpu.VMEM((length, kv_cols // 2), bf16),
            dma((pairs, others)),
            dma((pairs, others)),
            dma((pairs,)),
        ],
        compiler_params=pltpu.CompilerParams(
            collective_id=1, has_side_effects=True, vmem_limit_bytes=VMEM_LIMIT
        ),
        name="attend",
    )(
        sequence.reshape(length, total),
        head_queries.reshape(length, q_cols),
        portion.reshape(-1, kv_cols),
        results,
        combine,
    )
    return (attention, routed)


def solution(mesh):
    placed = (
        P(("node", "local"), None),
        P("node", None),
        P(),
        P(("node", "local"), None),
        P("node", "local"),
        P(("node", "local"), None),
        P(("node", "local"), None),
        P(("node", "local"), None, None),
        P(("node", "local"), None, None),
        P(("node", "local"), None, None),
    )
    return jax.shard_map(
        functools.partial(shards, mesh.shape["node"], mesh.shape["local"]),
        mesh=mesh,
        in_specs=placed,
        out_specs=(P(("node", "local"), None), P(("node", "local"), None)),
        check_vma=False,
    )
```

time: 335 us -> 146 us (0.44)
  waiting for transfers between devices: 145 us -> 0 us
  Pallas kernels: 0 us -> 136 us
  local copies, waits for them, and re-layouts: 85.3 us -> 4.52 us
  matrix products: 36.5 us -> 0.14 us
  starting transfers between devices: 19.5 us -> 0 us
  blocking collectives: 14.4 us -> 0 us
  between operations: 14.4 us -> 0.76 us
  other arithmetic: 16.2 us -> 4.03 us
    pallas_call x0 -> x2, Pallas kernels: none -> 136 us  [the longest x1 104 us: shards(): pl.pallas_call(body, out_shape=(jax.ShapeDtypeStruct((n_local, tokens, to...]
    all_to_all x4 -> x0, waiting for transfers between devices: 81.9 us -> none  [the longest x1 56.5 us: send_rows(): lax.all_to_all(buffer, ('node', 'local'), split_axis=0, concat_axis=0, ti...]
    all_gather x2 -> x0, waiting for transfers between devices: 61.9 us -> none  [the longest x1 61.9 us: shards(): portion = lax.all_gather(kv_weight, 'node', axis=0, tiled=True)]
    dot_general x52 -> x1, matrix products: 36.5 us -> 0.14 us  [shards(): slot = jnp.dot(earlier, member.astype(bf16), preferred_element_type=f32)]
    all_to_all x4 -> x0, starting transfers between devices: 19.5 us -> none  [the longest x1 6.9 us: send_rows(): lax.all_to_all(buffer, ('node', 'local'), split_axis=0, concat_axis=0, ti...]
    gather x9 -> x0, local copies, waits for them, and re-layouts: 17.6 us -> none  [the longest x8 16.4 us: shards(): results[route_index[:, column]].astype(jnp.float32)]
    dynamic_slice x32 -> x0, local copies, waits for them, and re-layouts: 17.2 us -> none  [shards(): lax.map(lambda head_pair: attend_head(head_pair[0], head_pair[1], keys_ro...]
    squeeze x16 -> x0, local copies, waits for them, and re-layouts: 15.6 us -> none  [shards(): lax.map(lambda head_pair: attend_head(head_pair[0], head_pair[1], keys_ro...]
  transfers between devices with their start and end apart: 6 -> 0, of which waited for: 4 -> 0; matrix products, arithmetic and copies ran while one was open for 38% -> 0% of each run, Pallas kernels for 0% -> 0%
where the time goes in v1:
time: 146 us
  Pallas kernels  136 us (93%)
  local copies, waits for them, and re-layouts  4.52 us (3%)
  other arithmetic  4.03 us (3%)
    pallas_call x1, Pallas kernels, shards(): pl.pallas_call(body, out_shape=(jax.ShapeDtypeStruct((n_local, tokens, to...  104 us
    pallas_call x1, Pallas kernels, shards(): pl.pallas_call(functools.partial(second_kernel, n_node, n_local), out_sha...  32.6 us
    unnamed x4, local copies, waits for them, and re-layouts  4.1 us

profile of v1, /device:TPU:1, one launch (start us, length us, event | category | flops | bytes accessed | tf_op | source)
XLA Modules:
  0.0 145.9 jit_solution(12679224319181925434)
XLA Ops:
  0.7 0.8 compare_reduce_fusion
  1.5 0.8 fusion
  2.2 0.1 eq.65
  2.3 0.1 fusion.4
  2.5 0.1 copy.27
  2.6 0.7 fusion.5.refs_1_
  3.3 0.1 copy.26
  3.4 0.1 copy.28
  3.6 0.7 pad_maximum_fusion.combine
  4.2 0.3 fusion.6
  4.6 0.8 pad_maximum_fusion.1
  5.3 103.8 %exchange.1 = (bf16[4,128,576]{2,1,0:T(8,128)(2,1)}, bf16[4,128,3072]{2,1,0:T(8,128)(2,1)}, bf16[8,64,4096]{2,1,0:T(8,128)(2,1)}, bf16[16,8,3584]{2,1,0:T(8,128)(2,1)}) custom-call(bf16[128,3584]{1,0:T(8,128)(2,1)} %refs_0_.1, bf16[128,128]{1,0:T(8,128)(2,1)} %fusion.5.refs_1_, f32[1,512]{1,0:T(1,128)} %bitcast.28, f32[128,64]{1,0:T(8,128)} %get-tuple-element.17.refs_3_, ...), custom_call_target="tpu_custom_call" | custom-call | tf_op jit(solution)/shard_map/exchange/pallas_call | solution.py:564
  109.2 32.6 %attend.1 = (bf16[128,8192]{1,0:T(8,128)(2,1)}, bf16[128,3584]{1,0:T(8,128)(2,1)}) custom-call(bf16[512,576]{1,0:T(8,128)(2,1)} %bitcast.27, bf16[512,3072]{1,0:T(8,128)(2,1)} %bitcast.26, bf16[512,4096]{1,0:T(8,128)(2,1)} %bitcast.25, bf16[16,8,3584]{2,1,0:T(8,128)(2,1)} %get-tuple-element.9.results, bf16[3,128,128]{2,1,0:T(8,128)(2,1)} %pad_maximum_fusion.combine), custom_call_target="tpu_custom_call" | custom-call | tf_op jit(solution)/shard_map/attend/pallas_call | solution.py:596
  141.8 0.0 copy-start
  141.8 3.2 %copy.31 = bf16[128,8192]{1,0:T(8,128)(2,1)} copy(bf16[128,8192]{1,0:T(8,128)(2,1)} %get-tuple-element.21) | data formatting | bytes 4194304
  144.9 0.0 copy-done
  144.9 0.9 copy.32
  (10 shorter events, 0.1 us)
Async XLA Ops:
  141.8 3.2 %copy-start = (bf16[128,3584]{1,0:T(8,128)(2,1)S(1)}, bf16[128,3584]{1,0:T(8,128)(2,1)}, u32[]{:S(2)}) copy-start(bf16[128,3584]{1,0:T(8,128)(2,1)} %get-tuple-element.22) | copy-start | bytes 2752516

commit v2 on v0

v2 whole, which is shorter than its diff:
```python
import functools
import math
import types

import jax
import jax.numpy as jnp
import numpy as np
from jax import lax
from jax.experimental import pallas as pl
from jax.experimental.pallas import tpu as pltpu
from jax.sharding import PartitionSpec as P

NOPE = 128
ROPE = 64
VDIM = 128
LAT = 512
EXPERTS = 256
CAP = 8
PAIR_Q = 2 * (NOPE + ROPE)
PAIR_KV = 2 * (NOPE + VDIM)
PAIR_V = 2 * VDIM
MESH = pl.DeviceIdType.MESH
VMEM_LIMIT = 56 * 2**20


def remote(src, dst, send_sem, recv_sem, device):
    return pltpu.make_async_remote_copy(
        src_ref=src,
        dst_ref=dst,
        send_sem=send_sem,
        recv_sem=recv_sem,
        device_id=device,
        device_id_type=MESH,
    )


def greet(devices, n_local, me):
    barrier = pltpu.get_barrier_semaphore()

    def signal(d, carry):
        other = lax.rem(me + d, devices)
        pl.semaphore_signal(
            barrier,
            inc=1,
            device_id=(lax.div(other, n_local), lax.rem(other, n_local)),
            device_id_type=MESH,
        )
        return carry

    lax.fori_loop(1, devices, signal, 0)
    pl.semaphore_wait(barrier, devices - 1)


class Gather:
    def __init__(self, own, slot, nz, ny, node, local, sems):
        self.own, self.slot, self.nz, self.ny = own, slot, nz, ny
        self.z, self.y, self.local = lax.div(node, ny), lax.rem(node, ny), local
        self.up_s, self.up_r, self.dn_s, self.dn_r, self.y_s, self.y_r = sems

    def up(self, h, src):
        z = jnp.maximum(self.z - h, 0)
        dst = self.slot(z * self.ny + self.y)
        to = jnp.minimum(self.z + 1, self.nz - 1)
        return remote(
            dst if src is None else src, dst, self.up_s.at[h], self.up_r.at[h], (to * self.ny + self.y, self.local)
        )

    def down(self, h, src):
        z = jnp.minimum(self.z + h, self.nz - 1)
        dst = self.slot(z * self.ny + self.y)
        to = jnp.maximum(self.z - 1, 0)
        return remote(
            dst if src is None else src, dst, self.dn_s.at[h], self.dn_r.at[h], (to * self.ny + self.y, self.local)
        )

    def across(self, z, dy, src):
        dst = self.slot(z * self.ny + self.y)
        to = self.z * self.ny + lax.rem(self.y + dy, self.ny)
        return remote(
            dst if src is None else src, dst, self.y_s.at[z, dy - 1], self.y_r.at[z, dy - 1], (to, self.local)
        )

    def begin(self):
        @pl.when(self.z < self.nz - 1)
        def _():
            self.up(0, self.own).start()

        @pl.when(self.z > 0)
        def _():
            self.down(0, self.own).start()

        for dy in range(1, self.ny):
            self.across(self.z, dy, self.own).start()

    def hop(self, h, landed=None):
        @pl.when(self.z - h >= 0)
        def _():
            self.up(h - 1, None).wait_recv()
            if h < self.nz - 1:

                @pl.when(self.z < self.nz - 1)
                def _():
                    self.up(h, None).start()

            for dy in range(1, self.ny):
                self.across(self.z - h, dy, None).start()
            if landed:
                landed((self.z - h) * self.ny + self.y)

        @pl.when(self.z + h < self.nz)
        def _():
            self.down(h - 1, None).wait_recv()
            if h < self.nz - 1:

                @pl.when(self.z > 0)
                def _():
                    self.down(h, None).start()

            for dy in range(1, self.ny):
                self.across(self.z + h, dy, None).start()
            if landed:
                landed((self.z + h) * self.ny + self.y)

    def columns(self, landed=None):
        for z in range(self.nz):
            for dy in range(1, self.ny):
                self.across(z, dy, None).wait_recv()
                if landed:
                    landed(z * self.ny + lax.rem(self.y - dy + self.ny, self.ny))

    def finish(self):
        for h in range(self.nz - 1):

            @pl.when((self.z < self.nz - 1) & (self.z - h >= 0))
            def _():
                self.up(h, None).wait_send()

            @pl.when((self.z > 0) & (self.z + h < self.nz))
            def _():
                self.down(h, None).wait_send()

        for z in range(self.nz):
            for dy in range(1, self.ny):
                self.across(z, dy, None).wait_send()


def present_routes(ids, gates, tokens, chips, stride):
    shape = (tokens, chips * CAP)
    lane = lax.broadcasted_iota(jnp.int32, shape, 1)
    expert = lax.div(lane, CAP) * stride
    count = jnp.zeros(shape, jnp.float32)
    weight = jnp.zeros(shape, jnp.float32)
    for k in range(ids.shape[1]):
        hit = ids[:, k : k + 1] == expert
        count += jnp.where(hit, 1.0, 0.0)
        weight += jnp.where(hit, gates[:, k : k + 1], 0.0)
    square = (tokens, tokens)
    earlier = lax.broadcasted_iota(jnp.int32, square, 1) < lax.broadcasted_iota(
        jnp.int32, square, 0
    )
    slot = jnp.dot(
        jnp.where(earlier, 1.0, 0.0).astype(jnp.bfloat16),
        count.astype(jnp.bfloat16),
        preferred_element_type=jnp.float32,
    )
    chosen = jnp.where(slot == lax.rem(lane, CAP).astype(jnp.float32), count, 0.0)
    return chosen, chosen * weight


def block_kernel(n_node, n_local, nz, stride, r):
    node, local = lax.axis_index("node"), lax.axis_index("local")
    devices, ny = n_node * n_local, n_node // nz
    chips = devices // 2
    me = node * n_local + local
    chip, core = lax.div(me, 2), lax.rem(me, 2)
    sibling = (node, local + 1 - 2 * core)
    half = r.lat.shape[2]
    tokens = r.hidden.shape[0]
    q_cols = r.q.shape[2]
    length = n_local * tokens
    pairs = r.kv.shape[2] // PAIR_KV
    wide = r.kv.shape[2] // 2
    front = pairs // 2

    own_q = pl.ds(pl.multiple_of(local * q_cols, 128), q_cols)
    weights_in = [
        pltpu.make_async_copy(r.gate_w.at[0], r.gates, r.local_sem.at[0]),
        pltpu.make_async_copy(r.up_w.at[0], r.ups, r.local_sem.at[1]),
        pltpu.make_async_copy(r.down_w.at[0], r.downs, r.local_sem.at[2]),
    ]
    kv_in = pltpu.make_async_copy(r.kv_w, r.kv.at[node], r.local_sem.at[3])
    q_in = pltpu.make_async_copy(r.queries.at[:, own_q], r.q.at[local], r.local_sem.at[4])
    lat_in = [
        pltpu.make_async_copy(
            r.latent_w.at[pl.ds(i * half, half)], r.lat.at[node, i], r.local_sem.at[5 + i]
        )
        for i in range(2)
    ]

    greet(devices, n_local, me)

    def device_of(c):
        dev = c * 2 + core
        return (lax.div(dev, n_local), lax.rem(dev, n_local))

    def go(d):
        to = lax.rem(chip + d, chips)
        return remote(
            r.leaving.at[to],
            r.arrived.at[core, chip],
            r.go_s.at[d - 1],
            r.go_r.at[d - 1],
            device_of(to),
        )

    def back(d):
        to = lax.rem(chip + d, chips)
        return remote(
            r.part.at[core, to],
            r.results.at[chip],
            r.back_s.at[d - 1],
            r.back_r.at[d - 1],
            device_of(to),
        )

    def each(first, last, act):
        def step(d, carry):
            act(d)
            return carry

        lax.fori_loop(first, last, step, 0)

    def ask(d):
        to = lax.rem(local + d, n_local)
        cols = pl.ds(pl.multiple_of(to * q_cols, 128), q_cols)
        return remote(
            r.queries.at[:, cols], r.q.at[local], r.q_s.at[d - 1], r.q_r.at[d - 1], (node, to)
        )

    lat_gather = Gather(
        r.latent_w.at[pl.ds(pl.multiple_of(core * half, 16), half)],
        lambda n: r.lat.at[n, core],
        nz,
        ny,
        node,
        local,
        r.lat_sems,
    )
    near = pl.ds(0, front * PAIR_KV)
    far = pl.ds(front * PAIR_KV, (pairs - front) * PAIR_KV)
    kv_near = Gather(
        r.kv_w.at[:, near], lambda n: r.kv.at[n, :, near], nz, ny, node, local, r.near_sems
    )
    kv_far = Gather(
        r.kv_w.at[:, far], lambda n: r.kv.at[n, :, far], nz, ny, node, local, r.far_sems
    )

    def share(n):
        return remote(
            r.lat.at[n, core], r.lat.at[n, core], r.core_s.at[n], r.core_r.at[n], sibling
        )

    def landed(n):
        share(n).start()

    lat_gather.begin()
    kv_near.begin()
    for d in range(1, n_local):
        ask(d).start()
    for copy in (*lat_in, kv_in, q_in, *weights_in):
        copy.start()

    chosen, dense = present_routes(r.ids, r.route_w, tokens, chips, stride)
    r.dense[...] = dense
    rows = lax.dot_general(
        chosen.astype(jnp.bfloat16),
        r.hidden[...],
        (((0,), (0,)), ((), ())),
        preferred_element_type=jnp.float32,
    )
    r.leaving[...] = rows.reshape(r.leaving.shape).astype(jnp.bfloat16)
    r.arrived[core, chip] = r.leaving[chip]

    for h in range(1, nz):
        lat_gather.hop(h, landed)
        kv_near.hop(h)
        if h == max(nz - 2, 1):
            each(1, chips, lambda d: go(d).start())
    kv_far.begin()

    lat_gather.columns(landed)

    def shared(n, carry):
        @pl.when(n != node)
        def _():
            remote(
                r.lat.at[n, 1 - core],
                r.lat.at[n, 1 - core],
                r.core_s.at[n],
                r.core_r.at[n],
                sibling,
            ).wait_recv()

        return carry

    lax.fori_loop(0, n_node, shared, 0)
    for copy in lat_in:
        copy.wait()
    weight = r.lat[...].reshape(n_node * 2 * half, r.lat.shape[3])
    latent = jnp.dot(r.hidden[...], weight, preferred_element_type=jnp.float32)
    u = latent[:, :LAT]
    norm = lax.rsqrt(jnp.mean(u * u, axis=1, keepdims=True) + 1e-06)
    r.mine[:, :LAT] = (u * norm * r.gain[...]).astype(jnp.bfloat16)
    a = latent[:, LAT:]
    swapped = jnp.concatenate([a[:, ROPE // 2 :], a[:, : ROPE // 2]], axis=1)
    turn = r.turns[pl.ds(pl.multiple_of(local * tokens, 16), tokens)]
    r.mine[:, LAT:] = (a * turn[:, :ROPE] + swapped * turn[:, ROPE:]).astype(jnp.bfloat16)

    def tell(d):
        to = lax.rem(local + d, n_local)
        return remote(
            r.mine, r.seq.at[local], r.seq_s.at[d - 1], r.seq_r.at[d - 1], (node, to)
        )

    for d in range(1, n_local):
        tell(d).start()
    r.seq[local] = r.mine[...]

    if nz > 1:
        kv_far.hop(1)
    kv_near.columns()
    kv_in.wait()
    q_in.wait()
    for d in range(1, n_local):
        ask(d).wait()
        tell(d).wait()

    scale = math.log2(math.e) / math.sqrt(NOPE + ROPE)
    step = 256
    diagonal = lax.broadcasted_iota(jnp.int32, (step, step), 1) <= lax.broadcasted_iota(
        jnp.int32, (step, step), 0
    )

    def place(p):
        return pl.ds(pl.multiple_of(local * wide + p * PAIR_V, 128), PAIR_V)

    def out_cols(p):
        return pl.ds(pl.multiple_of(p * PAIR_V, 128), PAIR_V)

    def reply(p, d):
        to = lax.rem(local + d, n_local)
        rows = pl.ds(pl.multiple_of(to * tokens, 16), tokens)
        return remote(
            r.outs.at[rows, out_cols(p)],
            r.attention.at[:, place(p)],
            r.out_s.at[p, d - 1],
            r.out_r.at[p, d - 1],
            (node, to),
        )

    def keep(p):
        rows = pl.ds(pl.multiple_of(local * tokens, 16), tokens)
        return pltpu.make_async_copy(
            r.outs.at[rows, out_cols(p)], r.attention.at[:, place(p)], r.keep.at[p]
        )

    def pair(p, carry):
        cols = pl.ds(pl.multiple_of(p * PAIR_KV, 128), PAIR_KV)
        compressed = r.seq[:, :, :LAT].reshape(length, LAT)
        rope = r.seq[:, :, LAT:].reshape(length, ROPE).astype(jnp.float32)
        zeros = jnp.zeros((length, 128 - ROPE), jnp.float32)
        up = r.kv[:, :, cols].reshape(LAT, PAIR_KV)
        keyval = jnp.dot(compressed, up, preferred_element_type=jnp.float32)
        first = jnp.concatenate([keyval[:, :NOPE], rope, zeros], axis=1).astype(jnp.bfloat16)
        at = NOPE + VDIM
        second = jnp.concatenate([zeros, keyval[:, at : at + NOPE], rope], axis=1).astype(
            jnp.bfloat16
        )
        for h, keys in enumerate((first, second)):
            values = keyval[:, h * at + NOPE : (h + 1) * at].astype(jnp.bfloat16)
            window = pl.ds(pl.multiple_of(p * PAIR_Q + h * 128, 128), 256)
            asked = r.q[:, :, window].reshape(length, 256)
            for b in range(length // step):
                end = (b + 1) * step
                scores = lax.dot_general(
                    asked[b * step : end],
                    keys[:end],
                    (((1,), (1,)), ((), ())),
                    preferred_element_type=jnp.float32,
                )
                last = jnp.where(diagonal, scores[:, b * step :], -1e30)
                scores = jnp.concatenate([scores[:, : b * step], last], axis=1) if b else last
                weights = jnp.exp2((scores - jnp.max(scores, axis=1, keepdims=True)) * scale)
                probs = (weights * (1.0 / jnp.sum(weights, axis=1, keepdims=True))).astype(
                    jnp.bfloat16
                )
                out = jnp.dot(probs, values[:end], preferred_element_type=jnp.float32)
                spot = pl.ds(pl.multiple_of(p * PAIR_V + h * VDIM, 128), VDIM)
                r.outs[b * step : end, spot] = out.astype(jnp.bfloat16)
        for d in range(1, n_local):
            reply(p, d).start()
        keep(p).start()
        return carry

    early = max(front // 2, 1)
    lax.fori_loop(0, early, pair, 0)
    if nz > 2:
        kv_far.hop(2)
    lax.fori_loop(early, front, pair, 0)
    for h in range(3, nz):
        kv_far.hop(h)

    each(1, chips, lambda d: go(d).wait_recv())
    swap = remote(
        r.arrived.at[core], r.arrived.at[core], r.sib_s.at[0], r.sib_r.at[0], sibling
    )
    swap.start()
    for copy in weights_in:
        copy.wait()
    swap.wait()

    batch = min(32, chips)
    per = chips // batch

    def expert(i, carry):
        c, p = lax.div(i, per), lax.rem(i, per)
        at = pl.ds(p * batch, batch)
        x = r.arrived[c, at].astype(jnp.float32).reshape(batch * CAP, -1).astype(jnp.bfloat16)
        gate = jnp.dot(x, r.gates[...], preferred_element_type=jnp.float32)
        upper = jnp.dot(x, r.ups[...], preferred_element_type=jnp.float32)
        inner = (gate / (1.0 + jnp.exp(-gate)) * upper).astype(jnp.bfloat16)
        width = r.downs.shape[1] // 7
        for j in range(7):
            cols = slice(j * width, (j + 1) * width)
            y = jnp.dot(inner, r.downs[:, cols], preferred_element_type=jnp.float32)
            r.part[c, at, :, cols] = y.reshape(batch, CAP, width).astype(jnp.bfloat16)
        return carry

    lax.fori_loop(0, 2 * per, expert, 0)
    give = remote(r.part.at[1 - core], r.sibpart, r.sib_s.at[1], r.sib_r.at[1], sibling)
    give.start()
    kv_far.columns()
    give.wait()

    def total(p, carry):
        both = r.part[core, p].astype(jnp.float32) + r.sibpart[p].astype(jnp.float32)
        r.part[core, p] = both.astype(jnp.bfloat16)
        return carry

    lax.fori_loop(0, chips, total, 0)
    each(1, chips, lambda d: back(d).start())
    r.results[chip] = r.part[core, chip]

    lax.fori_loop(front, pairs, pair, 0)

    each(1, chips, lambda d: back(d).wait())
    dense = r.dense[...]
    high = dense.astype(jnp.bfloat16)
    rest = dense - high.astype(jnp.float32)
    middle = rest.astype(jnp.bfloat16)
    low = (rest - middle.astype(jnp.float32)).astype(jnp.bfloat16)
    width = r.results.shape[2] // 7
    for j in range(7):
        cols = slice(j * width, (j + 1) * width)
        rows = (
            r.results[:, :, cols]
            .astype(jnp.float32)
            .reshape(chips * CAP, width)
            .astype(jnp.bfloat16)
        )
        sums = jnp.dot(high, rows, preferred_element_type=jnp.float32)
        sums += jnp.dot(middle, rows, preferred_element_type=jnp.float32)
        sums += jnp.dot(low, rows, preferred_element_type=jnp.float32)
        r.routed[:, cols] = sums.astype(jnp.bfloat16)

    each(1, chips, lambda d: go(d).wait_send())
    lat_gather.finish()
    kv_near.finish()
    kv_far.finish()

    def shared_sent(n, carry):
        @pl.when(n != node)
        def _():
            share(n).wait_send()

        return carry

    lax.fori_loop(0, n_node, shared_sent, 0)

    def settle(p, carry):
        for d in range(1, n_local):
            reply(p, d).wait()
        keep(p).wait()
        return carry

    lax.fori_loop(0, pairs, settle, 0)


def shards(
    n_node,
    n_local,
    hidden,
    latent_weight,
    latent_gain,
    queries,
    kv_weight,
    expert_ids,
    route_weights,
    gate_proj,
    up_proj,
    down_proj,
):
    tokens, width = hidden.shape
    chips = n_node * n_local // 2
    nz = 4 if n_node % 4 == 0 else n_node
    ny = n_node // nz
    bf16, f32 = jnp.bfloat16, jnp.float32
    length = n_local * tokens

    freqs = 10000.0 ** (-2.0 * np.arange(ROPE // 2) / ROPE)
    angles = np.arange(length)[:, None] * freqs[None, :]
    cosine, sine = np.cos(angles), np.sin(angles)
    turns = jnp.asarray(np.concatenate([cosine, cosine, -sine, sine], axis=1), f32)

    half = latent_weight.shape[0] // 2
    total = latent_weight.shape[1]
    kv_rows, kv_cols = kv_weight.shape
    q_cols = queries.shape[1] // n_local
    pairs = kv_cols // PAIR_KV
    vmem, hbm = pl.BlockSpec(memory_space=pltpu.VMEM), pl.BlockSpec(memory_space=pl.ANY)
    dma = pltpu.SemaphoreType.DMA
    chain = max(nz - 1, 1)
    gather = [dma((chain,))] * 4 + [dma((nz, max(ny - 1, 1)))] * 2
    others = max(n_local - 1, 1)
    width_e = gate_proj.shape[2]
    operands = dict(
        hidden=hidden,
        ids=expert_ids,
        route_w=route_weights,
        gain=latent_gain.reshape(1, -1),
        turns=turns,
        latent_w=latent_weight,
        queries=queries,
        kv_w=kv_weight,
        gate_w=gate_proj,
        up_w=up_proj,
        down_w=down_proj,
    )
    scratch = dict(
        lat=pltpu.VMEM((n_node, 2, half, total), bf16),
        kv=pltpu.VMEM((n_node, kv_rows, kv_cols), bf16),
        q=pltpu.VMEM((n_local, tokens, q_cols), bf16),
        seq=pltpu.VMEM((n_local, tokens, total), bf16),
        outs=pltpu.VMEM((length, kv_cols // 2), bf16),
        gates=pltpu.VMEM((width, width_e), bf16),
        ups=pltpu.VMEM((width, width_e), bf16),
        downs=pltpu.VMEM((width_e, width), bf16),
        leaving=pltpu.VMEM((chips, CAP, width), bf16),
        arrived=pltpu.VMEM((2, chips, CAP, width), bf16),
        part=pltpu.VMEM((2, chips, CAP, width), bf16),
        sibpart=pltpu.VMEM((chips, CAP, width), bf16),
        results=pltpu.VMEM((chips, CAP, width), bf16),
        mine=pltpu.VMEM((tokens, total), bf16),
        dense=pltpu.VMEM((tokens, chips * CAP), f32),
        local_sem=dma((7,)),
        core_s=dma((n_node,)),
        core_r=dma((n_node,)),
        q_s=dma((others,)),
        q_r=dma((others,)),
        seq_s=dma((others,)),
        seq_r=dma((others,)),
        go_s=dma((chips - 1,)),
        go_r=dma((chips - 1,)),
        back_s=dma((chips - 1,)),
        back_r=dma((chips - 1,)),
        sib_s=dma((2,)),
        sib_r=dma((2,)),
        out_s=dma((pairs, others)),
        out_r=dma((pairs, others)),
        keep=dma((pairs,)),
    )
    names = [*operands, "attention", "routed", *scratch]

    def body(*refs):
        r = types.SimpleNamespace(**dict(zip(names, refs)))
        rest = refs[len(names) :]
        r.lat_sems, r.near_sems, r.far_sems = rest[:6], rest[6:12], rest[12:]
        block_kernel(n_node, n_local, nz, EXPERTS // chips, r)

    return pl.pallas_call(
        body,
        out_shape=(
            jax.ShapeDtypeStruct((tokens, n_local * kv_cols // 2), bf16),
            jax.ShapeDtypeStruct((tokens, width), bf16),
        ),
        in_specs=[vmem] * 5 + [hbm] * 6,
        out_specs=(hbm, vmem),
        scratch_shapes=[*scratch.values(), *gather * 3],
        compiler_params=pltpu.CompilerParams(
            collective_id=0, has_side_effects=True, vmem_limit_bytes=VMEM_LIMIT
        ),
        name="block",
    )(*operands.values())


def solution(mesh):
    placed = (
        P(("node", "local"), None),
        P("node", None),
        P(),
        P(("node", "local"), None),
        P("node", "local"),
        P(("node", "local"), None),
        P(("node", "local"), None),
        P(("node", "local"), None, None),
        P(("node", "local"), None, None),
        P(("node", "local"), None, None),
    )
    return jax.shard_map(
        functools.partial(shards, mesh.shape["node"], mesh.shape["local"]),
        mesh=mesh,
        in_specs=placed,
        out_specs=(P(("node", "local"), None), P(("node", "local"), None)),
        check_vma=False,
    )
```

time: 335 us -> 123 us (0.37)
  waiting for transfers between devices: 145 us -> 0 us
  Pallas kernels: 0 us -> 114 us
  local copies, waits for them, and re-layouts: 85.3 us -> 6.93 us
  matrix products: 36.5 us -> 0 us
  starting transfers between devices: 19.5 us -> 0 us
  other arithmetic: 16.2 us -> 0 us
  blocking collectives: 14.4 us -> 0 us
  between operations: 14.4 us -> 0.65 us
    pallas_call x0 -> x1, Pallas kernels: none -> 114 us  [shards(): pl.pallas_call(body, out_shape=(jax.ShapeDtypeStruct((tokens, n_local * k...]
    all_to_all x4 -> x0, waiting for transfers between devices: 81.9 us -> none  [the longest x1 56.5 us: send_rows(): lax.all_to_all(buffer, ('node', 'local'), split_axis=0, concat_axis=0, ti...]
    all_gather x2 -> x0, waiting for transfers between devices: 61.9 us -> none  [the longest x1 61.9 us: shards(): portion = lax.all_gather(kv_weight, 'node', axis=0, tiled=True)]
    dot_general x52 -> x0, matrix products: 36.5 us -> none  [the longest x1 7.2 us: expert_half(): jnp.dot(inner, down_proj[0], preferred_element_type=jnp.float32)]
    all_to_all x4 -> x0, starting transfers between devices: 19.5 us -> none  [the longest x1 6.9 us: send_rows(): lax.all_to_all(buffer, ('node', 'local'), split_axis=0, concat_axis=0, ti...]
    gather x9 -> x0, local copies, waits for them, and re-layouts: 17.6 us -> none  [the longest x8 16.4 us: shards(): results[route_index[:, column]].astype(jnp.float32)]
    dynamic_slice x32 -> x0, local copies, waits for them, and re-layouts: 17.2 us -> none  [shards(): lax.map(lambda head_pair: attend_head(head_pair[0], head_pair[1], keys_ro...]
    squeeze x16 -> x0, local copies, waits for them, and re-layouts: 15.6 us -> none  [shards(): lax.map(lambda head_pair: attend_head(head_pair[0], head_pair[1], keys_ro...]
  transfers between devices with their start and end apart: 6 -> 0, of which waited for: 4 -> 0; matrix products, arithmetic and copies ran while one was open for 38% -> 0% of each run, Pallas kernels for 0% -> 0%
where the time goes in v2:
time: 123 us; the launch traced here: 122 us
  Pallas kernels  114 us (93%)
  local copies, waits for them, and re-layouts  6.93 us (6%)
    pallas_call x1, Pallas kernels, shards(): pl.pallas_call(body, out_shape=(jax.ShapeDtypeStruct((tokens, n_local * k...  114 us
    unnamed x6, local copies, waits for them, and re-layouts  6.93 us

profile of v2, /device:TPU:1, one launch (start us, length us, event | category | flops | bytes accessed | tf_op | source)
XLA Modules:
  0.0 121.9 jit_solution(8387311113265123103)
XLA Ops:
  0.6 1.4 %copy.13.refs_1_ = s32[128,8]{1,0:T(8,128)} copy(s32[128,8]{0,1:T(8,128)} %param.16) | data formatting | bytes 8192 | tf_op args[5]
  2.0 1.4 %copy.14.refs_2_ = f32[128,8]{1,0:T(8,128)} copy(f32[128,8]{0,1:T(8,128)} %param.17) | data formatting | bytes 8192 | tf_op args[6]
  3.5 114.3 %block.1 = (bf16[128,8192]{1,0:T(8,128)(2,1)}, bf16[128,3584]{1,0:T(8,128)(2,1)}) custom-call(bf16[128,3584]{1,0:T(8,128)(2,1)} %refs_0_.1, s32[128,8]{1,0:T(8,128)} %copy.13.refs_1_, f32[128,8]{1,0:T(8,128)} %copy.14.refs_2_, f32[1,512]{1,0:T(1,128)} %bitcast.1, f32[512,128]{1,0:T(8,128)} %constant.2.clone.refs_4_, bf16[448,576]{1,0:T(8,128)(2,1)} %refs_5_.1, ...), custom_call_target="tpu_custom_call" | custom-call | tf_op jit(solution)/shard_map/block/pallas_call | solution.py:590
  117.8 0.0 copy-start
  117.8 3.2 %copy.17 = bf16[128,8192]{1,0:T(8,128)(2,1)} copy(bf16[128,8192]{1,0:T(8,128)(2,1)} %get-tuple-element.4) | data formatting | bytes 4194304
  121.0 0.0 copy-done
  121.0 0.9 copy.18
Async XLA Ops:
  117.8 3.2 %copy-start = (bf16[128,3584]{1,0:T(8,128)(2,1)S(1)}, bf16[128,3584]{1,0:T(8,128)(2,1)}, u32[]{:S(2)}) copy-start(bf16[128,3584]{1,0:T(8,128)(2,1)} %get-tuple-element.5) | copy-start | bytes 2752516

commit v3 on v2

--- a/solution.py
+++ b/solution.py
@@ -145,25 +145,25 @@
 
 
 def present_routes(ids, gates, tokens, chips, stride):
-    shape = (tokens, chips * CAP)
-    lane = lax.broadcasted_iota(jnp.int32, shape, 1)
-    expert = lax.div(lane, CAP) * stride
+    shape = (chips * CAP, tokens)
+    row = lax.broadcasted_iota(jnp.int32, shape, 0)
+    expert = lax.div(row, CAP) * stride
     count = jnp.zeros(shape, jnp.float32)
     weight = jnp.zeros(shape, jnp.float32)
-    for k in range(ids.shape[1]):
-        hit = ids[:, k : k + 1] == expert
+    for k in range(ids.shape[0]):
+        hit = ids[k : k + 1, :] == expert
         count += jnp.where(hit, 1.0, 0.0)
-        weight += jnp.where(hit, gates[:, k : k + 1], 0.0)
+        weight += jnp.where(hit, gates[k : k + 1, :], 0.0)
     square = (tokens, tokens)
-    earlier = lax.broadcasted_iota(jnp.int32, square, 1) < lax.broadcasted_iota(
-        jnp.int32, square, 0
+    earlier = lax.broadcasted_iota(jnp.int32, square, 0) < lax.broadcasted_iota(
+        jnp.int32, square, 1
     )
     slot = jnp.dot(
+        count.astype(jnp.bfloat16),
         jnp.where(earlier, 1.0, 0.0).astype(jnp.bfloat16),
-        count.astype(jnp.bfloat16),
         preferred_element_type=jnp.float32,
     )
-    chosen = jnp.where(slot == lax.rem(lane, CAP).astype(jnp.float32), count, 0.0)
+    chosen = jnp.where(slot == lax.rem(row, CAP).astype(jnp.float32), count, 0.0)
     return chosen, chosen * weight
 
 
@@ -197,6 +197,17 @@
         for i in range(2)
     ]
 
+    for copy in (*lat_in, kv_in, q_in, *weights_in):
+        copy.start()
+
+    chosen, dense = present_routes(r.ids, r.route_w, tokens, chips, stride)
+    r.dense[...] = dense
+    rows = jnp.dot(
+        chosen.astype(jnp.bfloat16), r.hidden[...], preferred_element_type=jnp.float32
+    )
+    r.leaving[...] = rows.reshape(r.leaving.shape).astype(jnp.bfloat16)
+    r.arrived[core, chip] = r.leaving[chip]
+
     greet(devices, n_local, me)
 
     def device_of(c):
@@ -264,31 +275,22 @@
         share(n).start()
 
     lat_gather.begin()
+    each(1, chips, lambda d: go(d).start())
     kv_near.begin()
     for d in range(1, n_local):
         ask(d).start()
-    for copy in (*lat_in, kv_in, q_in, *weights_in):
-        copy.start()
-
-    chosen, dense = present_routes(r.ids, r.route_w, tokens, chips, stride)
-    r.dense[...] = dense
-    rows = lax.dot_general(
-        chosen.astype(jnp.bfloat16),
-        r.hidden[...],
-        (((0,), (0,)), ((), ())),
-        preferred_element_type=jnp.float32,
-    )
-    r.leaving[...] = rows.reshape(r.leaving.shape).astype(jnp.bfloat16)
-    r.arrived[core, chip] = r.leaving[chip]
 
     for h in range(1, nz):
         lat_gather.hop(h, landed)
         kv_near.hop(h)
-        if h == max(nz - 2, 1):
-            each(1, chips, lambda d: go(d).start())
     kv_far.begin()
 
     lat_gather.columns(landed)
+    each(1, chips, lambda d: go(d).wait_recv())
+    swap = remote(
+        r.arrived.at[core], r.arrived.at[core], r.sib_s.at[0], r.sib_r.at[0], sibling
+    )
+    swap.start()
 
     def shared(n, carry):
         @pl.when(n != node)
@@ -328,6 +330,47 @@
 
     if nz > 1:
         kv_far.hop(1)
+
+    for copy in weights_in:
+        copy.wait()
+    swap.wait()
+
+    batch = min(32, chips)
+    per = chips // batch
+
+    def expert(i, carry):
+        c, p = lax.div(i, per), lax.rem(i, per)
+        at = pl.ds(p * batch, batch)
+        x = r.arrived[c, at].astype(jnp.float32).reshape(batch * CAP, -1).astype(jnp.bfloat16)
+        gate = jnp.dot(x, r.gates[...], preferred_element_type=jnp.float32)
+        upper = jnp.dot(x, r.ups[...], preferred_element_type=jnp.float32)
+        inner = (gate / (1.0 + jnp.exp(-gate)) * upper).astype(jnp.bfloat16)
+        width = r.downs.shape[1] // 7
+        for j in range(7):
+            cols = slice(j * width, (j + 1) * width)
+            y = jnp.dot(inner, r.downs[:, cols], preferred_element_type=jnp.float32)
+            r.part[c, at, :, cols] = y.reshape(batch, CAP, width).astype(jnp.bfloat16)
+        return carry
+
+    lax.fori_loop(0, 2 * per, expert, 0)
+    give = remote(r.part.at[1 - core], r.sibpart, r.sib_s.at[1], r.sib_r.at[1], sibling)
+    give.start()
+    if nz > 2:
+        kv_far.hop(2)
+    give.wait()
+
+    def total(p, carry):
+        both = r.part[core, p].astype(jnp.float32) + r.sibpart[p].astype(jnp.float32)
+        r.part[core, p] = both.astype(jnp.bfloat16)
+        return carry
+
+    lax.fori_loop(0, chips, total, 0)
+    each(1, chips, lambda d: back(d).start())
+    kept = pltpu.make_async_copy(r.part.at[core, chip], r.results.at[chip], r.local_sem.at[7])
+    kept.start()
+    for h in range(3, nz):
+        kv_far.hop(h)
+
     kv_near.columns()
     kv_in.wait()
     q_in.wait()
@@ -369,6 +412,7 @@
         compressed = r.seq[:, :, :LAT].reshape(length, LAT)
         rope = r.seq[:, :, LAT:].reshape(length, ROPE).astype(jnp.float32)
         zeros = jnp.zeros((length, 128 - ROPE), jnp.float32)
+        ones = jnp.ones((length, VDIM), jnp.bfloat16)
         up = r.kv[:, :, cols].reshape(LAT, PAIR_KV)
         keyval = jnp.dot(compressed, up, preferred_element_type=jnp.float32)
         first = jnp.concatenate([keyval[:, :NOPE], rope, zeros], axis=1).astype(jnp.bfloat16)
@@ -377,7 +421,9 @@
             jnp.bfloat16
         )
         for h, keys in enumerate((first, second)):
-            values = keyval[:, h * at + NOPE : (h + 1) * at].astype(jnp.bfloat16)
+            values = jnp.concatenate(
+                [keyval[:, h * at + NOPE : (h + 1) * at].astype(jnp.bfloat16), ones], axis=1
+            )
             window = pl.ds(pl.multiple_of(p * PAIR_Q + h * 128, 128), 256)
             asked = r.q[:, :, window].reshape(length, 256)
             for b in range(length // step):
@@ -391,10 +437,10 @@
                 last = jnp.where(diagonal, scores[:, b * step :], -1e30)
                 scores = jnp.concatenate([scores[:, : b * step], last], axis=1) if b else last
                 weights = jnp.exp2((scores - jnp.max(scores, axis=1, keepdims=True)) * scale)
-                probs = (weights * (1.0 / jnp.sum(weights, axis=1, keepdims=True))).astype(
-                    jnp.bfloat16
+                both = jnp.dot(
+                    weights.astype(jnp.bfloat16), values[:end], preferred_element_type=jnp.float32
                 )
-                out = jnp.dot(probs, values[:end], preferred_element_type=jnp.float32)
+                out = both[:, :VDIM] / both[:, VDIM:]
                 spot = pl.ds(pl.multiple_of(p * PAIR_V + h * VDIM, 128), VDIM)
                 r.outs[b * step : end, spot] = out.astype(jnp.bfloat16)
         for d in range(1, n_local):
@@ -402,77 +448,12 @@
         keep(p).start()
         return carry
 
-    early = max(front // 2, 1)
-    lax.fori_loop(0, early, pair, 0)
-    if nz > 2:
-        kv_far.hop(2)
-    lax.fori_loop(early, front, pair, 0)
-    for h in range(3, nz):
-        kv_far.hop(h)
-
-    each(1, chips, lambda d: go(d).wait_recv())
-    swap = remote(
-        r.arrived.at[core], r.arrived.at[core], r.sib_s.at[0], r.sib_r.at[0], sibling
-    )
-    swap.start()
-    for copy in weights_in:
-        copy.wait()
-    swap.wait()
-
-    batch = min(32, chips)
-    per = chips // batch
-
-    def expert(i, carry):
-        c, p = lax.div(i, per), lax.rem(i, per)
-        at = pl.ds(p * batch, batch)
-        x = r.arrived[c, at].astype(jnp.float32).reshape(batch * CAP, -1).astype(jnp.bfloat16)
-        gate = jnp.dot(x, r.gates[...], preferred_element_type=jnp.float32)
-        upper = jnp.dot(x, r.ups[...], preferred_element_type=jnp.float32)
-        inner = (gate / (1.0 + jnp.exp(-gate)) * upper).astype(jnp.bfloat16)
-        width = r.downs.shape[1] // 7
-        for j in range(7):
-            cols = slice(j * width, (j + 1) * width)
-            y = jnp.dot(inner, r.downs[:, cols], preferred_element_type=jnp.float32)
-            r.part[c, at, :, cols] = y.reshape(batch, CAP, width).astype(jnp.bfloat16)
-        return carry
-
-    lax.fori_loop(0, 2 * per, expert, 0)
-    give = remote(r.part.at[1 - core], r.sibpart, r.sib_s.at[1], r.sib_r.at[1], sibling)
-    give.start()
+    lax.fori_loop(0, front, pair, 0)
     kv_far.columns()
-    give.wait()
-
-    def total(p, carry):
-        both = r.part[core, p].astype(jnp.float32) + r.sibpart[p].astype(jnp.float32)
-        r.part[core, p] = both.astype(jnp.bfloat16)
-        return carry
-
-    lax.fori_loop(0, chips, total, 0)
-    each(1, chips, lambda d: back(d).start())
-    r.results[chip] = r.part[core, chip]
-
     lax.fori_loop(front, pairs, pair, 0)
 
     each(1, chips, lambda d: back(d).wait())
-    dense = r.dense[...]
-    high = dense.astype(jnp.bfloat16)
-    rest = dense - high.astype(jnp.float32)
-    middle = rest.astype(jnp.bfloat16)
-    low = (rest - middle.astype(jnp.float32)).astype(jnp.bfloat16)
-    width = r.results.shape[2] // 7
-    for j in range(7):
-        cols = slice(j * width, (j + 1) * width)
-        rows = (
-            r.results[:, :, cols]
-            .astype(jnp.float32)
-            .reshape(chips * CAP, width)
-            .astype(jnp.bfloat16)
-        )
-        sums = jnp.dot(high, rows, preferred_element_type=jnp.float32)
-        sums += jnp.dot(middle, rows, preferred_element_type=jnp.float32)
-        sums += jnp.dot(low, rows, preferred_element_type=jnp.float32)
-        r.routed[:, cols] = sums.astype(jnp.bfloat16)
-
+    kept.wait()
     each(1, chips, lambda d: go(d).wait_send())
     lat_gather.finish()
     kv_near.finish()
@@ -494,6 +475,42 @@
         return carry
 
     lax.fori_loop(0, pairs, settle, 0)
+
+
+def finish_kernel(arrived, results, dense, attention, routed, sem):
+    rows = arrived.shape[0] // 4
+    copies = [
+        pltpu.make_async_copy(
+            arrived.at[pl.ds(i * rows, rows)], attention.at[pl.ds(i * rows, rows)], sem.at[i]
+        )
+        for i in range(4)
+    ]
+    for copy in copies:
+        copy.start()
+    chips = results.shape[0]
+    weight = dense[...]
+    high = weight.astype(jnp.bfloat16)
+    rest = weight - high.astype(jnp.float32)
+    middle = rest.astype(jnp.bfloat16)
+    low = (rest - middle.astype(jnp.float32)).astype(jnp.bfloat16)
+    width = results.shape[2] // 7
+    for j in range(7):
+        cols = slice(j * width, (j + 1) * width)
+        rows = (
+            results[:, :, cols]
+            .astype(jnp.float32)
+            .reshape(chips * CAP, width)
+            .astype(jnp.bfloat16)
+        )
+        sums = [
+            lax.dot_general(
+                term, rows, (((0,), (0,)), ((), ())), preferred_element_type=jnp.float32
+            )
+            for term in (high, middle, low)
+        ]
+        routed[:, cols] = (sums[0] + sums[1] + sums[2]).astype(jnp.bfloat16)
+    for copy in copies:
+        copy.wait()
 
 
 def shards(
@@ -535,8 +552,8 @@
     width_e = gate_proj.shape[2]
     operands = dict(
         hidden=hidden,
-        ids=expert_ids,
-        route_w=route_weights,
+        ids=expert_ids.T,
+        route_w=route_weights.T,
         gain=latent_gain.reshape(1, -1),
         turns=turns,
         latent_w=latent_weight,
@@ -559,10 +576,8 @@
         arrived=pltpu.VMEM((2, chips, CAP, width), bf16),
         part=pltpu.VMEM((2, chips, CAP, width), bf16),
         sibpart=pltpu.VMEM((chips, CAP, width), bf16),
-        results=pltpu.VMEM((chips, CAP, width), bf16),
         mine=pltpu.VMEM((tokens, total), bf16),
-        dense=pltpu.VMEM((tokens, chips * CAP), f32),
-        local_sem=dma((7,)),
+        local_sem=dma((8,)),
         core_s=dma((n_node,)),
         core_r=dma((n_node,)),
         q_s=dma((others,)),
@@ -579,7 +594,7 @@
         out_r=dma((pairs, others)),
         keep=dma((pairs,)),
     )
-    names = [*operands, "attention", "routed", *scratch]
+    names = [*operands, "attention", "results", "dense", *scratch]
 
     def body(*refs):
         r = types.SimpleNamespace(**dict(zip(names, refs)))
@@ -587,20 +602,33 @@
         r.lat_sems, r.near_sems, r.far_sems = rest[:6], rest[6:12], rest[12:]
         block_kernel(n_node, n_local, nz, EXPERTS // chips, r)
 
-    return pl.pallas_call(
+    attention, results, dense = pl.pallas_call(
         body,
         out_shape=(
             jax.ShapeDtypeStruct((tokens, n_local * kv_cols // 2), bf16),
-            jax.ShapeDtypeStruct((tokens, width), bf16),
+            jax.ShapeDtypeStruct((chips, CAP, width), bf16),
+            jax.ShapeDtypeStruct((chips * CAP, tokens), f32),
         ),
         in_specs=[vmem] * 5 + [hbm] * 6,
-        out_specs=(hbm, vmem),
+        out_specs=(hbm, hbm, vmem),
         scratch_shapes=[*scratch.values(), *gather * 3],
         compiler_params=pltpu.CompilerParams(
             collective_id=0, has_side_effects=True, vmem_limit_bytes=VMEM_LIMIT
         ),
         name="block",
     )(*operands.values())
+    return pl.pallas_call(
+        finish_kernel,
+        out_shape=(
+            jax.ShapeDtypeStruct(attention.shape, bf16),
+            jax.ShapeDtypeStruct((tokens, width), bf16),
+        ),
+        in_specs=[hbm, vmem, vmem],
+        out_specs=(hbm, vmem),
+        scratch_shapes=[dma((4,))],
+        compiler_params=pltpu.CompilerParams(vmem_limit_bytes=VMEM_LIMIT),
+        name="finish",
+    )(attention, results, dense)
 
 
 def solution(mesh):

time: 123 us -> 183 us (1.49)
  Pallas kernels: 114 us -> 182 us
  local copies, waits for them, and re-layouts: 6.93 us -> 0 us
    pallas_call x0 -> x1, Pallas kernels: none -> 66.8 us  [shards(): pl.pallas_call(finish_kernel, out_shape=(jax.ShapeDtypeStruct(attention.s...]
    unnamed x6 -> x0, local copies, waits for them, and re-layouts: 6.93 us -> none
where the time goes in v3:
time: 183 us
  Pallas kernels  182 us (99%)
    pallas_call x1, Pallas kernels, shards(): pl.pallas_call(body, out_shape=(jax.ShapeDtypeStruct((tokens, n_local * k...  115 us
    pallas_call x1, Pallas kernels, shards(): pl.pallas_call(finish_kernel, out_shape=(jax.ShapeDtypeStruct(attention.s...  66.8 us

profile of v3, /device:TPU:1, one launch (start us, length us, event | category | flops | bytes accessed | tf_op | source)
XLA Modules:
  0.0 182.5 jit_solution(11496092259647696122)
XLA Ops:
  0.6 115.1 %block.1 = (bf16[128,8192]{1,0:T(8,128)(2,1)}, bf16[16,8,3584]{2,1,0:T(8,128)(2,1)}, f32[128,128]{1,0:T(8,128)}) custom-call(bf16[128,3584]{1,0:T(8,128)(2,1)} %refs_0_.1, s32[8,128]{1,0:T(8,128)} %bitcast.3, f32[8,128]{1,0:T(8,128)} %bitcast.4, f32[1,512]{1,0:T(1,128)} %bitcast.5, f32[512,128]{1,0:T(8,128)} %constant.2.clone.refs_4_, ...), custom_call_target="tpu_custom_call" | custom-call | tf_op jit(solution)/shard_map/block/pallas_call | solution.py:605
  115.8 66.8 %finish.1 = (bf16[128,8192]{1,0:T(8,128)(2,1)}, bf16[128,3584]{1,0:T(8,128)(2,1)}) custom-call(bf16[128,8192]{1,0:T(8,128)(2,1)} %get-tuple-element.5.arrived, bf16[16,8,3584]{2,1,0:T(8,128)(2,1)} %get-tuple-element.6.results, f32[128,128]{1,0:T(8,128)} %get-tuple-element.7.dense), custom_call_target="tpu_custom_call" | custom-call | tf_op jit(solution)/shard_map/finish/pallas_call | solution.py:620

commit v4 on v3

--- a/solution.py
+++ b/solution.py
@@ -180,7 +180,8 @@
     length = n_local * tokens
     pairs = r.kv.shape[2] // PAIR_KV
     wide = r.kv.shape[2] // 2
-    front = pairs // 2
+    parts = len(r.kv_sems)
+    front = pairs // parts
 
     own_q = pl.ds(pl.multiple_of(local * q_cols, 128), q_cols)
     weights_in = [
@@ -206,7 +207,8 @@
         chosen.astype(jnp.bfloat16), r.hidden[...], preferred_element_type=jnp.float32
     )
     r.leaving[...] = rows.reshape(r.leaving.shape).astype(jnp.bfloat16)
-    r.arrived[core, chip] = r.leaving[chip]
+    r.arrived[core * chips + chip] = r.leaving[chip]
+    mine_blocks = pl.ds(core * chips, chips)
 
     greet(devices, n_local, me)
 
@@ -218,7 +220,7 @@
         to = lax.rem(chip + d, chips)
         return remote(
             r.leaving.at[to],
-            r.arrived.at[core, chip],
+            r.arrived.at[core * chips + chip],
             r.go_s.at[d - 1],
             r.go_r.at[d - 1],
             device_of(to),
@@ -227,7 +229,7 @@
     def back(d):
         to = lax.rem(chip + d, chips)
         return remote(
-            r.part.at[core, to],
+            r.part.at[core * chips + to],
             r.results.at[chip],
             r.back_s.at[d - 1],
             r.back_r.at[d - 1],
@@ -257,14 +259,13 @@
         local,
         r.lat_sems,
     )
-    near = pl.ds(0, front * PAIR_KV)
-    far = pl.ds(front * PAIR_KV, (pairs - front) * PAIR_KV)
-    kv_near = Gather(
-        r.kv_w.at[:, near], lambda n: r.kv.at[n, :, near], nz, ny, node, local, r.near_sems
-    )
-    kv_far = Gather(
-        r.kv_w.at[:, far], lambda n: r.kv.at[n, :, far], nz, ny, node, local, r.far_sems
-    )
+    def part_of_kv(i):
+        cols = pl.ds(i * front * PAIR_KV, front * PAIR_KV)
+        return Gather(
+            r.kv_w.at[:, cols], lambda n: r.kv.at[n, :, cols], nz, ny, node, local, r.kv_sems[i]
+        )
+
+    kv_parts = [part_of_kv(i) for i in range(parts)]
 
     def share(n):
         return remote(
@@ -274,23 +275,59 @@
     def landed(n):
         share(n).start()
 
+    def wave(step):
+        if step < nz:
+            lat_gather.hop(step, landed)
+        for i, gather in enumerate(kv_parts):
+            if step == i:
+                gather.begin()
+            elif 1 <= step - i < nz:
+                gather.hop(step - i)
+
+    waves = nz + parts - 1
     lat_gather.begin()
     each(1, chips, lambda d: go(d).start())
-    kv_near.begin()
+    kv_parts[0].begin()
     for d in range(1, n_local):
         ask(d).start()
 
-    for h in range(1, nz):
-        lat_gather.hop(h, landed)
-        kv_near.hop(h)
-    kv_far.begin()
-
-    lat_gather.columns(landed)
+    wave(1)
     each(1, chips, lambda d: go(d).wait_recv())
     swap = remote(
-        r.arrived.at[core], r.arrived.at[core], r.sib_s.at[0], r.sib_r.at[0], sibling
+        r.arrived.at[mine_blocks], r.arrived.at[mine_blocks], r.sib_s.at[0], r.sib_r.at[0], sibling
     )
     swap.start()
+    wave(2)
+    for copy in weights_in:
+        copy.wait()
+    swap.wait()
+    batch = min(32, 2 * chips)
+
+    def expert(i, carry):
+        at = pl.ds(i * batch, batch)
+        x = r.arrived[at].astype(jnp.float32).reshape(batch * CAP, -1).astype(jnp.bfloat16)
+        gate = jnp.dot(x, r.gates[...], preferred_element_type=jnp.float32)
+        upper = jnp.dot(x, r.ups[...], preferred_element_type=jnp.float32)
+        inner = (gate / (1.0 + jnp.exp(-gate)) * upper).astype(jnp.bfloat16)
+        width = r.downs.shape[1] // 7
+        for j in range(7):
+            cols = slice(j * width, (j + 1) * width)
+            y = jnp.dot(inner, r.downs[:, cols], preferred_element_type=jnp.float32)
+            r.part[at, :, cols] = y.reshape(batch, CAP, width).astype(jnp.bfloat16)
+        return carry
+
+    lax.fori_loop(0, 2 * chips // batch, expert, 0)
+    give = remote(
+        r.part.at[pl.ds((1 - core) * chips, chips)],
+        r.sibpart,
+        r.sib_s.at[1],
+        r.sib_r.at[1],
+        sibling,
+    )
+    give.start()
+    wave(3)
+
+    lat_gather.columns(landed)
 
     def shared(n, carry):
         @pl.when(n != node)
@@ -328,50 +365,21 @@
         tell(d).start()
     r.seq[local] = r.mine[...]
 
-    if nz > 1:
-        kv_far.hop(1)
-
-    for copy in weights_in:
-        copy.wait()
-    swap.wait()
-
-    batch = min(32, chips)
-    per = chips // batch
-
-    def expert(i, carry):
-        c, p = lax.div(i, per), lax.rem(i, per)
-        at = pl.ds(p * batch, batch)
-        x = r.arrived[c, at].astype(jnp.float32).reshape(batch * CAP, -1).astype(jnp.bfloat16)
-        gate = jnp.dot(x, r.gates[...], preferred_element_type=jnp.float32)
-        upper = jnp.dot(x, r.ups[...], preferred_element_type=jnp.float32)
-        inner = (gate / (1.0 + jnp.exp(-gate)) * upper).astype(jnp.bfloat16)
-        width = r.downs.shape[1] // 7
-        for j in range(7):
-            cols = slice(j * width, (j + 1) * width)
-            y = jnp.dot(inner, r.downs[:, cols], preferred_element_type=jnp.float32)
-            r.part[c, at, :, cols] = y.reshape(batch, CAP, width).astype(jnp.bfloat16)
+    wave(4)
+    give.wait()
+
+    def total(p, carry):
+        at = core * chips + p
+        both = r.part[at].astype(jnp.float32) + r.sibpart[p].astype(jnp.float32)
+        r.part[at] = both.astype(jnp.bfloat16)
         return carry
 
-    lax.fori_loop(0, 2 * per, expert, 0)
-    give = remote(r.part.at[1 - core], r.sibpart, r.sib_s.at[1], r.sib_r.at[1], sibling)
-    give.start()
-    if nz > 2:
-        kv_far.hop(2)
-    give.wait()
-
-    def total(p, carry):
-        both = r.part[core, p].astype(jnp.float32) + r.sibpart[p].astype(jnp.float32)
-        r.part[core, p] = both.astype(jnp.bfloat16)
-        return carry
-
     lax.fori_loop(0, chips, total, 0)
-    each(1, chips, lambda d: back(d).start())
-    kept = pltpu.make_async_copy(r.part.at[core, chip], r.results.at[chip], r.local_sem.at[7])
+    kept = pltpu.make_async_copy(
+        r.part.at[core * chips + chip], r.results.at[chip], r.local_sem.at[7]
+    )
     kept.start()
-    for h in range(3, nz):
-        kv_far.hop(h)
-
-    kv_near.columns()
+
     kv_in.wait()
     q_in.wait()
     for d in range(1, n_local):
@@ -448,16 +456,20 @@
         keep(p).start()
         return carry
 
-    lax.fori_loop(0, front, pair, 0)
-    kv_far.columns()
-    lax.fori_loop(front, pairs, pair, 0)
+    for i in range(parts):
+        kv_parts[i].columns()
+        lax.fori_loop(i * front, (i + 1) * front, pair, 0)
+        if i + 5 < waves:
+            wave(i + 5)
+        if i == 0:
+            each(1, chips, lambda d: back(d).start())
 
     each(1, chips, lambda d: back(d).wait())
     kept.wait()
     each(1, chips, lambda d: go(d).wait_send())
     lat_gather.finish()
-    kv_near.finish()
-    kv_far.finish()
+    for gather in kv_parts:
+        gather.finish()
 
     def shared_sent(n, carry):
         @pl.when(n != node)
@@ -477,40 +489,22 @@
     lax.fori_loop(0, pairs, settle, 0)
 
 
-def finish_kernel(arrived, results, dense, attention, routed, sem):
-    rows = arrived.shape[0] // 4
-    copies = [
-        pltpu.make_async_copy(
-            arrived.at[pl.ds(i * rows, rows)], attention.at[pl.ds(i * rows, rows)], sem.at[i]
-        )
-        for i in range(4)
-    ]
-    for copy in copies:
-        copy.start()
+def finish_kernel(arrived, results, dense, attention, routed):
+    attention[...] = arrived[...]
     chips = results.shape[0]
     weight = dense[...]
     high = weight.astype(jnp.bfloat16)
     rest = weight - high.astype(jnp.float32)
     middle = rest.astype(jnp.bfloat16)
     low = (rest - middle.astype(jnp.float32)).astype(jnp.bfloat16)
-    width = results.shape[2] // 7
-    for j in range(7):
-        cols = slice(j * width, (j + 1) * width)
-        rows = (
-            results[:, :, cols]
-            .astype(jnp.float32)
-            .reshape(chips * CAP, width)
-            .astype(jnp.bfloat16)
-        )
-        sums = [
-            lax.dot_general(
-                term, rows, (((0,), (0,)), ((), ())), preferred_element_type=jnp.float32
-            )
-            for term in (high, middle, low)
-        ]
-        routed[:, cols] = (sums[0] + sums[1] + sums[2]).astype(jnp.bfloat16)
-    for copy in copies:
-        copy.wait()
+    rows = (
+        results[...].astype(jnp.float32).reshape(chips * CAP, -1).astype(jnp.bfloat16)
+    )
+    sums = [
+        lax.dot_general(term, rows, (((0,), (0,)), ((), ())), preferred_element_type=jnp.float32)
+        for term in (high, middle, low)
+    ]
+    routed[...] = (sums[0] + sums[1] + sums[2]).astype(jnp.bfloat16)
 
 
 def shards(
@@ -573,8 +567,8 @@
         ups=pltpu.VMEM((width, width_e), bf16),
         downs=pltpu.VMEM((width_e, width), bf16),
         leaving=pltpu.VMEM((chips, CAP, width), bf16),
-        arrived=pltpu.VMEM((2, chips, CAP, width), bf16),
-        part=pltpu.VMEM((2, chips, CAP, width), bf16),
+        arrived=pltpu.VMEM((2 * chips, CAP, width), bf16),
+        part=pltpu.VMEM((2 * chips, CAP, width), bf16),
         sibpart=pltpu.VMEM((chips, CAP, width), bf16),
         mine=pltpu.VMEM((tokens, total), bf16),
         local_sem=dma((8,)),
@@ -599,7 +593,8 @@
     def body(*refs):
         r = types.SimpleNamespace(**dict(zip(names, refs)))
         rest = refs[len(names) :]
-        r.lat_sems, r.near_sems, r.far_sems = rest[:6], rest[6:12], rest[12:]
+        r.lat_sems = rest[:6]
+        r.kv_sems = [rest[i : i + 6] for i in range(6, len(rest), 6)]
         block_kernel(n_node, n_local, nz, EXPERTS // chips, r)
 
     attention, results, dense = pl.pallas_call(
@@ -611,21 +606,29 @@
         ),
         in_specs=[vmem] * 5 + [hbm] * 6,
         out_specs=(hbm, hbm, vmem),
-        scratch_shapes=[*scratch.values(), *gather * 3],
+        scratch_shapes=[*scratch.values(), *gather * (1 + min(4, pairs))],
         compiler_params=pltpu.CompilerParams(
             collective_id=0, has_side_effects=True, vmem_limit_bytes=VMEM_LIMIT
         ),
         name="block",
     )(*operands.values())
+    steps = 4
     return pl.pallas_call(
         finish_kernel,
         out_shape=(
             jax.ShapeDtypeStruct(attention.shape, bf16),
             jax.ShapeDtypeStruct((tokens, width), bf16),
         ),
-        in_specs=[hbm, vmem, vmem],
-        out_specs=(hbm, vmem),
-        scratch_shapes=[dma((4,))],
+        grid=(steps,),
+        in_specs=[
+            pl.BlockSpec((tokens, attention.shape[1] // steps), lambda i: (0, i)),
+            pl.BlockSpec((chips, CAP, width // steps), lambda i: (0, 0, i)),
+            pl.BlockSpec(dense.shape, lambda i: (0, 0)),
+        ],
+        out_specs=(
+            pl.BlockSpec((tokens, attention.shape[1] // steps), lambda i: (0, i)),
+            pl.BlockSpec((tokens, width // steps), lambda i: (0, i)),
+        ),
         compiler_params=pltpu.CompilerParams(vmem_limit_bytes=VMEM_LIMIT),
         name="finish",
     )(attention, results, dense)

time: 183 us -> 116 us (0.63)
  Pallas kernels: 182 us -> 115 us
    pallas_call x1, Pallas kernels: 66.8 us -> 4.65 us  [shards(): pl.pallas_call(finish_kernel, out_shape=(jax.ShapeDtypeStruct(attention.s...]
    pallas_call x1, Pallas kernels: 115 us -> 110 us  [shards(): pl.pallas_call(body, out_shape=(jax.ShapeDtypeStruct((tokens, n_local * k...]
where the time goes in v4:
time: 116 us
  Pallas kernels  115 us (99%)
    pallas_call x1, Pallas kernels, shards(): pl.pallas_call(body, out_shape=(jax.ShapeDtypeStruct((tokens, n_local * k...  110 us
    pallas_call x1, Pallas kernels, shards(): pl.pallas_call(finish_kernel, out_shape=(jax.ShapeDtypeStruct(attention.s...  4.65 us

profile of v4, /device:TPU:1, one launch (start us, length us, event | category | flops | bytes accessed | tf_op | source)
XLA Modules:
  0.0 115.7 jit_solution(16188918477583367755)
XLA Ops:
  0.6 110.4 %block.1 = (bf16[128,8192]{1,0:T(8,128)(2,1)}, bf16[16,8,3584]{2,1,0:T(8,128)(2,1)}, f32[128,128]{1,0:T(8,128)}) custom-call(bf16[128,3584]{1,0:T(8,128)(2,1)} %refs_0_.1, s32[8,128]{1,0:T(8,128)} %bitcast.3, f32[8,128]{1,0:T(8,128)} %bitcast.4, f32[1,512]{1,0:T(1,128)} %bitcast.5, f32[512,128]{1,0:T(8,128)} %constant.2.clone.refs_4_, ...), custom_call_target="tpu_custom_call" | custom-call | tf_op jit(solution)/shard_map/block/pallas_call | solution.py:600
  111.1 4.7 %finish.1 = (bf16[128,8192]{1,0:T(8,128)(2,1)}, bf16[128,3584]{1,0:T(8,128)(2,1)}) custom-call(bf16[128,8192]{1,0:T(8,128)(2,1)} %get-tuple-element.5.arrived, bf16[16,8,3584]{2,1,0:T(8,128)(2,1)} %get-tuple-element.6.results, f32[128,128]{1,0:T(8,128)} %get-tuple-element.7.dense), custom_call_target="tpu_custom_call" | custom-call | tf_op jit(solution)/shard_map/finish/pallas_call | solution.py:616

commit v5 on v4

--- a/solution.py
+++ b/solution.py
@@ -201,15 +201,6 @@
     for copy in (*lat_in, kv_in, q_in, *weights_in):
         copy.start()
 
-    chosen, dense = present_routes(r.ids, r.route_w, tokens, chips, stride)
-    r.dense[...] = dense
-    rows = jnp.dot(
-        chosen.astype(jnp.bfloat16), r.hidden[...], preferred_element_type=jnp.float32
-    )
-    r.leaving[...] = rows.reshape(r.leaving.shape).astype(jnp.bfloat16)
-    r.arrived[core * chips + chip] = r.leaving[chip]
-    mine_blocks = pl.ds(core * chips, chips)
-
     greet(devices, n_local, me)
 
     def device_of(c):
@@ -266,6 +257,8 @@
         )
 
     kv_parts = [part_of_kv(i) for i in range(parts)]
+    later = [0 if 2 * i < parts else 1 for i in range(parts)]
+    mine_blocks = pl.ds(core * chips, chips)
 
     def share(n):
         return remote(
@@ -279,17 +272,38 @@
         if step < nz:
             lat_gather.hop(step, landed)
         for i, gather in enumerate(kv_parts):
-            if step == i:
+            if step == later[i]:
                 gather.begin()
-            elif 1 <= step - i < nz:
-                gather.hop(step - i)
-
-    waves = nz + parts - 1
+            elif 1 <= step - later[i] < nz:
+                gather.hop(step - later[i])
+
     lat_gather.begin()
-    each(1, chips, lambda d: go(d).start())
-    kv_parts[0].begin()
+    for i in range(parts):
+        if later[i] == 0:
+            kv_parts[i].begin()
     for d in range(1, n_local):
         ask(d).start()
+
+    chosen, dense = present_routes(r.ids, r.route_w, tokens, chips, stride)
+    slots = chips * CAP
+    same = lax.broadcasted_iota(jnp.int32, (slots, slots), 0) == lax.broadcasted_iota(
+        jnp.int32, (slots, slots), 1
+    )
+    unit = jnp.where(same, 1.0, 0.0).astype(jnp.bfloat16)
+    for i in range(3):
+        term = dense.astype(jnp.bfloat16)
+        dense = dense - term.astype(jnp.float32)
+        turned = lax.dot_general(
+            term, unit, (((0,), (0,)), ((), ())), preferred_element_type=jnp.float32
+        )
+        r.terms[:, i * slots : (i + 1) * slots] = turned.astype(jnp.bfloat16)
+    rows = jnp.dot(
+        chosen.astype(jnp.bfloat16), r.hidden[...], preferred_element_type=jnp.float32
+    )
+    r.leaving[...] = rows.reshape(r.leaving.shape).astype(jnp.bfloat16)
+    r.arrived[core * chips + chip] = r.leaving[chip]
+
+    each(1, chips, lambda d: go(d).start())
 
     wave(1)
     each(1, chips, lambda d: go(d).wait_recv())
@@ -379,6 +393,7 @@
         r.part.at[core * chips + chip], r.results.at[chip], r.local_sem.at[7]
     )
     kept.start()
+    each(1, chips, lambda d: back(d).start())
 
     kv_in.wait()
     q_in.wait()
@@ -459,10 +474,6 @@
     for i in range(parts):
         kv_parts[i].columns()
         lax.fori_loop(i * front, (i + 1) * front, pair, 0)
-        if i + 5 < waves:
-            wave(i + 5)
-        if i == 0:
-            each(1, chips, lambda d: back(d).start())
 
     each(1, chips, lambda d: back(d).wait())
     kept.wait()
@@ -489,22 +500,19 @@
     lax.fori_loop(0, pairs, settle, 0)
 
 
-def finish_kernel(arrived, results, dense, attention, routed):
+def finish_kernel(arrived, results, terms, attention, routed):
     attention[...] = arrived[...]
     chips = results.shape[0]
-    weight = dense[...]
-    high = weight.astype(jnp.bfloat16)
-    rest = weight - high.astype(jnp.float32)
-    middle = rest.astype(jnp.bfloat16)
-    low = (rest - middle.astype(jnp.float32)).astype(jnp.bfloat16)
     rows = (
         results[...].astype(jnp.float32).reshape(chips * CAP, -1).astype(jnp.bfloat16)
     )
-    sums = [
-        lax.dot_general(term, rows, (((0,), (0,)), ((), ())), preferred_element_type=jnp.float32)
-        for term in (high, middle, low)
-    ]
-    routed[...] = (sums[0] + sums[1] + sums[2]).astype(jnp.bfloat16)
+    slots = chips * CAP
+    total = jnp.zeros(routed.shape, jnp.float32)
+    for i in range(3):
+        total += jnp.dot(
+            terms[:, i * slots : (i + 1) * slots], rows, preferred_element_type=jnp.float32
+        )
+    routed[...] = total.astype(jnp.bfloat16)
 
 
 def shards(
@@ -588,7 +596,7 @@
         out_r=dma((pairs, others)),
         keep=dma((pairs,)),
     )
-    names = [*operands, "attention", "results", "dense", *scratch]
+    names = [*operands, "attention", "results", "terms", *scratch]
 
     def body(*refs):
         r = types.SimpleNamespace(**dict(zip(names, refs)))
@@ -597,12 +605,12 @@
         r.kv_sems = [rest[i : i + 6] for i in range(6, len(rest), 6)]
         block_kernel(n_node, n_local, nz, EXPERTS // chips, r)
 
-    attention, results, dense = pl.pallas_call(
+    attention, results, terms = pl.pallas_call(
         body,
         out_shape=(
             jax.ShapeDtypeStruct((tokens, n_local * kv_cols // 2), bf16),
             jax.ShapeDtypeStruct((chips, CAP, width), bf16),
-            jax.ShapeDtypeStruct((chips * CAP, tokens), f32),
+            jax.ShapeDtypeStruct((tokens, 3 * chips * CAP), bf16),
         ),
         in_specs=[vmem] * 5 + [hbm] * 6,
         out_specs=(hbm, hbm, vmem),
@@ -623,7 +631,7 @@
         in_specs=[
             pl.BlockSpec((tokens, attention.shape[1] // steps), lambda i: (0, i)),
             pl.BlockSpec((chips, CAP, width // steps), lambda i: (0, 0, i)),
-            pl.BlockSpec(dense.shape, lambda i: (0, 0)),
+            pl.BlockSpec(terms.shape, lambda i: (0, 0)),
         ],
         out_specs=(
             pl.BlockSpec((tokens, attention.shape[1] // steps), lambda i: (0, i)),
@@ -631,7 +639,7 @@
         ),
         compiler_params=pltpu.CompilerParams(vmem_limit_bytes=VMEM_LIMIT),
         name="finish",
-    )(attention, results, dense)
+    )(attention, results, terms)
 
 
 def solution(mesh):

time: 116 us -> 129 us (1.11)
  Pallas kernels: 115 us -> 129 us
    pallas_call x1, Pallas kernels: 110 us -> 124 us  [shards(): pl.pallas_call(body, out_shape=(jax.ShapeDtypeStruct((tokens, n_local * k...]
where the time goes in v5:
time: 129 us
  Pallas kernels  129 us (100%)
    pallas_call x1, Pallas kernels, shards(): pl.pallas_call(body, out_shape=(jax.ShapeDtypeStruct((tokens, n_local * k...  124 us
    pallas_call x1, Pallas kernels, shards(): pl.pallas_call(finish_kernel, out_shape=(jax.ShapeDtypeStruct(attention.s...  4.57 us

profile of v5, /device:TPU:1, one launch (start us, length us, event | category | flops | bytes accessed | tf_op | source)
XLA Modules:
  0.0 129.2 jit_solution(16393541300413872231)
XLA Ops:
  0.6 124.0 %block.1 = (bf16[128,8192]{1,0:T(8,128)(2,1)}, bf16[16,8,3584]{2,1,0:T(8,128)(2,1)}, bf16[128,384]{1,0:T(8,128)(2,1)}) custom-call(bf16[128,3584]{1,0:T(8,128)(2,1)} %refs_0_.1, s32[8,128]{1,0:T(8,128)} %bitcast.3, f32[8,128]{1,0:T(8,128)} %bitcast.4, f32[1,512]{1,0:T(1,128)} %bitcast.5, f32[512,128]{1,0:T(8,128)} %constant.2.clone.refs_4_, ...), custom_call_target="tpu_custom_call" | custom-call | tf_op jit(solution)/shard_map/block/pallas_call | solution.py:608
  124.7 4.6 %finish.1 = (bf16[128,8192]{1,0:T(8,128)(2,1)}, bf16[128,3584]{1,0:T(8,128)(2,1)}) custom-call(bf16[128,8192]{1,0:T(8,128)(2,1)} %get-tuple-element.5.arrived, bf16[16,8,3584]{2,1,0:T(8,128)(2,1)} %get-tuple-element.6.results, bf16[128,384]{1,0:T(8,128)(2,1)} %get-tuple-element.7.terms), custom_call_target="tpu_custom_call" | custom-call | tf_op jit(solution)/shard_map/finish/pallas_call | solution.py:624

commit v6 on v4

--- a/solution.py
+++ b/solution.py
@@ -201,15 +201,7 @@
     for copy in (*lat_in, kv_in, q_in, *weights_in):
         copy.start()
 
-    chosen, dense = present_routes(r.ids, r.route_w, tokens, chips, stride)
-    r.dense[...] = dense
-    rows = jnp.dot(
-        chosen.astype(jnp.bfloat16), r.hidden[...], preferred_element_type=jnp.float32
-    )
-    r.leaving[...] = rows.reshape(r.leaving.shape).astype(jnp.bfloat16)
-    r.arrived[core * chips + chip] = r.leaving[chip]
     mine_blocks = pl.ds(core * chips, chips)
-
     greet(devices, n_local, me)
 
     def device_of(c):
@@ -286,6 +278,15 @@
 
     waves = nz + parts - 1
     lat_gather.begin()
+
+    chosen, dense = present_routes(r.ids, r.route_w, tokens, chips, stride)
+    r.dense[...] = dense
+    rows = jnp.dot(
+        chosen.astype(jnp.bfloat16), r.hidden[...], preferred_element_type=jnp.float32
+    )
+    r.leaving[...] = rows.reshape(r.leaving.shape).astype(jnp.bfloat16)
+    r.arrived[core * chips + chip] = r.leaving[chip]
+
     each(1, chips, lambda d: go(d).start())
     kv_parts[0].begin()
     for d in range(1, n_local):

time: 116 us -> 115 us (level)
  no operation moved by 1% of the time
where the time goes in v6:
time: 115 us
  Pallas kernels  114 us (99%)
    pallas_call x1, Pallas kernels, shards(): pl.pallas_call(body, out_shape=(jax.ShapeDtypeStruct((tokens, n_local * k...  110 us
    pallas_call x1, Pallas kernels, shards(): pl.pallas_call(finish_kernel, out_shape=(jax.ShapeDtypeStruct(attention.s...  4.68 us

profile of v6, /device:TPU:1, one launch (start us, length us, event | category | flops | bytes accessed | tf_op | source)
XLA Modules:
  0.0 115.1 jit_solution(18365454935755233448)
XLA Ops:
  0.6 109.8 %block.1 = (bf16[128,8192]{1,0:T(8,128)(2,1)}, bf16[16,8,3584]{2,1,0:T(8,128)(2,1)}, f32[128,128]{1,0:T(8,128)}) custom-call(bf16[128,3584]{1,0:T(8,128)(2,1)} %refs_0_.1, s32[8,128]{1,0:T(8,128)} %bitcast.3, f32[8,128]{1,0:T(8,128)} %bitcast.4, f32[1,512]{1,0:T(1,128)} %bitcast.5, f32[512,128]{1,0:T(8,128)} %constant.2.clone.refs_4_, ...), custom_call_target="tpu_custom_call" | custom-call | tf_op jit(solution)/shard_map/block/pallas_call | solution.py:601
  110.4 4.7 %finish.1 = (bf16[128,8192]{1,0:T(8,128)(2,1)}, bf16[128,3584]{1,0:T(8,128)(2,1)}) custom-call(bf16[128,8192]{1,0:T(8,128)(2,1)} %get-tuple-element.5.arrived, bf16[16,8,3584]{2,1,0:T(8,128)(2,1)} %get-tuple-element.6.results, f32[128,128]{1,0:T(8,128)} %get-tuple-element.7.dense), custom_call_target="tpu_custom_call" | custom-call | tf_op jit(solution)/shard_map/finish/pallas_call | solution.py:617
